TPU v7x, 32 devices: a whole 2x2x4 slice. The times are simulated.
32 devices in a mesh: row: 8 (over y, x, core), col: 4 (over z).
Axes of the slice: x: 2, y: 2, z: 4, core: 2. Of those that a mesh axis runs over, the one named last changes fastest.
Arguments:
- field: bfloat16 [32, 16, 32, 512], P('row', 'col'), may hold values from -6 to 6
- near_kernel: bfloat16 [9, 2, 2, 256, 256], replicated, may hold values from -0.09375 to 0.09375
- contact: int32 [32, 16, 9], P('row', 'col'), may hold values from 0 to 1
- pillar_shift: int32 [32, 16, 2], P('row', 'col'), may hold values from 0 to 15
- wave_index: int32 [2048, 2], replicated, may hold values from -16 to 15
- wave_form: bfloat16 [2048, 2, 256], replicated, may hold values from -0.25 to 0.25
- wave_weight: float32 [2048], replicated, may hold values from 0.5 to 4
Outputs:
- applied: float32 [32, 16, 32, 512], P('row', 'col')
All inputs are finite; a program needn't handle non-finite values.
Results may differ from a plain program's by a relative error of at most 0.0038.
Values may be sent and summed in bfloat16 or wider, within the bound.
No kernel may reach another device: no remote copies, remote signals or barrier semaphores. Data moves between devices by JAX's collectives and lax.ppermute only.
A program may use at most 128 MiB of HBM per device.

v0:
```python
import math

import jax
import jax.numpy as jnp
from jax import lax
from jax.sharding import PartitionSpec as P

Q = 16


bloch_row = 0.3
bloch_col = 0.17


def extended(cells, sides, width):
    for axis, dim in sides:
        count = lax.axis_size(axis)
        head = lax.slice_in_dim(cells, 0, width, axis=dim)
        tail = lax.slice_in_dim(cells, cells.shape[dim] - width, cells.shape[dim], axis=dim)
        cells = jnp.concatenate(
            [
                lax.ppermute(tail, axis, [(i, (i + 1) % count) for i in range(count)]),
                cells,
                lax.ppermute(head, axis, [((i + 1) % count, i) for i in range(count)]),
            ],
            axis=dim,
        )
    return cells


def realify(real_part, imag_part):
    upper = jnp.concatenate([real_part.T, imag_part.T], axis=1)
    lower = jnp.concatenate([-imag_part.T, real_part.T], axis=1)
    return jnp.concatenate([upper, lower], axis=0)


def wave_angle(wave_index, fine_row, fine_col, row_mod, col_mod):
    order_row = wave_index[:, 0:1]
    order_col = wave_index[:, 1:2]
    turn_row = jnp.mod(order_row * fine_row[None, :], row_mod).astype(jnp.float32) / row_mod
    turn_col = jnp.mod(order_col * fine_col[None, :], col_mod).astype(jnp.float32) / col_mod
    drift = (
        bloch_row * fine_row.astype(jnp.float32) / row_mod
        + bloch_col * fine_col.astype(jnp.float32) / col_mod
    )
    return 2.0 * math.pi * (turn_row + turn_col + drift[None, :])


def local(field, near_kernel, contact, pillar_shift, wave_index, wave_form, wave_weight):
    rows_here = field.shape[0]
    cols_here = field.shape[1]
    sources = field.shape[2]
    width = field.shape[3]
    waves = wave_form.shape[0]
    n_row = lax.axis_size("row")
    n_col = lax.axis_size("col")
    rows_total = rows_here * n_row
    cols_total = cols_here * n_col
    row_mod = Q * rows_total
    col_mod = Q * cols_total
    wave_matrix = realify(wave_form[:, 0], wave_form[:, 1])
    padded = extended(field, (("row", 0), ("col", 1)), 1)
    global_row = lax.axis_index("row") * rows_here + jnp.arange(rows_here, dtype=jnp.int32)
    global_col = lax.axis_index("col") * cols_here + jnp.arange(cols_here, dtype=jnp.int32)
    fine_row = (Q * global_row[:, None] + pillar_shift[:, :, 0]).reshape(-1)
    fine_col = (Q * global_col[None, :] + pillar_shift[:, :, 1]).reshape(-1)
    angles = wave_angle(wave_index, fine_row, fine_col, row_mod, col_mod)
    cos_all = jnp.cos(angles).T
    sin_all = jnp.sin(angles).T
    projected = jnp.dot(field.reshape(-1, width), wave_matrix, preferred_element_type=jnp.float32)
    projected = projected.reshape(rows_here * cols_here, sources, 2, waves)
    hi = lax.Precision.HIGHEST
    coeff_real = jnp.einsum("pw,psw->sw", cos_all, projected[:, :, 0], precision=hi) - jnp.einsum(
        "pw,psw->sw", sin_all, projected[:, :, 1], precision=hi
    )
    coeff_imag = jnp.einsum("pw,psw->sw", cos_all, projected[:, :, 1], precision=hi) + jnp.einsum(
        "pw,psw->sw", sin_all, projected[:, :, 0], precision=hi
    )
    partial_coeff = jnp.stack([coeff_real, coeff_imag], axis=1)
    near = jnp.zeros((rows_here, cols_here, sources, width), jnp.float32)
    for offset in range(9):
        step_row = offset // 3 - 1
        step_col = offset % 3 - 1
        block = padded[
            1 + step_row : 1 + step_row + rows_here, 1 + step_col : 1 + step_col + cols_here
        ]
        block = block.reshape(-1, width)
        for variant in range(near_kernel.shape[1]):
            near_mat = realify(near_kernel[offset, variant, 0], near_kernel[offset, variant, 1])
            product = jnp.dot(block, near_mat, preferred_element_type=jnp.float32).reshape(
                rows_here, cols_here, sources, width
            )
            chosen = (contact[:, :, offset] == variant)[:, :, None, None]
            near = near + jnp.where(chosen, product, jnp.float32(0.0))
    far_scale = math.sqrt(width // 2 / (waves * rows_total * cols_total))
    owned = lax.psum_scatter(partial_coeff, ("row", "col"), scatter_dimension=2, tiled=True)
    owner = lax.axis_index("row") * n_col + lax.axis_index("col")
    count = owned.shape[2]
    scales = far_scale * lax.dynamic_slice_in_dim(wave_weight, owner * owned.shape[2], count, 0)
    weighted = (scales[None, None, :] * owned).astype(jnp.bfloat16)
    add_weighted = lax.all_gather(weighted, ("row", "col"), axis=2, tiled=True)
    count = add_weighted.shape[2]
    cos_part = cos_all[:, None, :]
    sin_part = sin_all[:, None, :]
    weight_real = add_weighted[:, 0].astype(jnp.float32)[None]
    weight_imag = add_weighted[:, 1].astype(jnp.float32)[None]
    spread_real = cos_part * weight_real + sin_part * weight_imag
    spread_imag = cos_part * weight_imag - sin_part * weight_real
    spread = (
        jnp.concatenate([spread_real, spread_imag], axis=-1)
        .astype(jnp.bfloat16)
        .reshape(-1, 2 * count)
    )
    columns = jnp.concatenate(
        [
            lax.slice_in_dim(wave_matrix, 0, count, axis=1),
            lax.dynamic_slice_in_dim(wave_matrix, waves, count, 1),
        ],
        axis=1,
    )
    far = lax.dot_general(
        spread, columns, (((1,), (1,)), ((), ())), preferred_element_type=jnp.float32
    )
    return near + far.reshape(rows_here, cols_here, sources, width)


def solution(mesh):
    placed = (
        P("row", "col", None, None),
        P(),
        P("row", "col", None),
        P("row", "col", None),
        P(),
        P(),
        P(),
    )
    return jax.shard_map(
        local, mesh=mesh, in_specs=placed, out_specs=P("row", "col", None, None), check_vma=False
    )
```

profile of v0, /device:TPU:0, one launch (start us, length us, event | category | flops | bytes accessed | tf_op | source)
XLA Modules:
  0.0 312.1 jit_solution(4157783278226346596)
XLA Ops:
  6.5 6.5 %fusion.184 = (bf16[2048,1,256]{2,1,0:T(2,128)(2,1)S(1)}, bf16[2048,1,256]{2,1,0:T(2,128)(2,1)}) fusion(bf16[2048,2,256]{2,1,0:T(2,128)(2,1)} %param.12), kind=kLoop, calls=%fused_computation.309 | loop fusion | bytes 4194304 | tf_op jit(solution)/shard_map/slice | solution.py:61
  13.0 5.8 %copy.160 = bf16[2048,1,256]{0,2,1:T(8,128)(2,1)} copy(bf16[2048,1,256]{2,1,0:T(2,128)(2,1)} %get-tuple-element.78) | data formatting | bytes 2097152
  18.8 2.6 copy.161
  22.5 7.4 %convolution_bitcast_fusion = f32[512,4096]{0,1:T(8,128)} fusion(bf16[512,512]{1,0:T(8,128)(2,1)} %bitcast.290, bf16[256,2048]{1,0:T(8,128)(2,1)} %bitcast.293, bf16[256,2048]{1,0:T(8,128)(2,1)S(1)} %bitcast_negate_fusion, bf16[256,2048]{1,0:T(8,128)(2,1)S(1)} %bitcast.284), kind=kOutput, calls=%fused_computation | convolution fusion | flops 2164260864 | bytes 12058624 | tf_op jit(solution)/shard_map/dot_general | solution.py:70
  29.9 9.0 %copy.111 = f32[512,4096]{1,0:T(8,128)} copy(f32[512,4096]{0,1:T(8,128)} %convolution_bitcast_fusion) | data formatting | bytes 16777216 | tf_op jit(solution)/shard_map/dot_general | solution.py:70
  38.8 11.8 %reshape.488 = f32[16,32,2,2048]{3,2,1,0:T(2,128)} reshape(f32[512,4096]{1,0:T(8,128)} %copy.111) | data formatting | bytes 16777216 | tf_op jit(solution)/shard_map/reshape | solution.py:71
  50.6 12.2 %fusion.181 = (f32[16,32,1,2048]{3,2,1,0:T(1,128)}, f32[16,32,1,2048]{3,2,1,0:T(1,128)}) fusion(f32[16,32,2,2048]{3,2,1,0:T(2,128)} %reshape.488), kind=kLoop, calls=%fused_computation.306 | loop fusion | bytes 16777216 | tf_op jit(solution)/shard_map/slice | solution.py:74
  65.1 6.9 %fusion.6 = (f32[2048,32]{0,1:T(8,128)S(1)}, f32[2048,32]{0,1:T(8,128)S(1)}, f32[2048,32]{0,1:T(8,128)S(1)}, f32[2048,32]{0,1:T(8,128)S(1)}) fusion(f32[16,32,1,2048]{3,2,1,0:T(1,128)} %get-tuple-element.38, f32[2048,16]{0,1:T(8,128)S(1)} %get-tuple-element.97, f32[2048,16]{0,1:T(8,128)S(1)} %get-tuple-element.96, f32[16,32,1,2048]{3,2,1,0:T(1,128)} %get-tuple-element.37), kind=kLoop, calls=%fused_computation.12 | loop fusion | flops 8126464 | bytes 9699328 | tf_op jit(solution)/shard_map/pw,psw->sw/dot_general | solution.py:73
  72.9 2.6 copy.156
  75.5 2.1 reshape.516
  77.7 1.7 fusion.186
  79.8 2.9 collective-permute-start.1
  82.7 2.7 fusion.182
  85.4 2.9 fusion.183
  88.4 1.7 fusion.179
  90.8 1.6 bitcast_negate_fusion.1
  92.5 1.7 copy.191
  94.1 1.6 bitcast_negate_fusion.2
  95.7 1.7 copy.189
  97.4 1.6 bitcast_negate_fusion.3
  98.9 1.7 copy.187
  100.6 1.6 bitcast_negate_fusion.4
  102.2 1.7 copy.185
  103.8 1.6 bitcast_negate_fusion.5
  105.4 1.7 copy.183
  107.1 1.6 bitcast_negate_fusion.6
  108.6 1.7 copy.181
  110.3 1.6 bitcast_negate_fusion.7
  112.6 1.6 bitcast_negate_fusion.9
  115.0 1.0 copy.173
  116.7 1.0 copy.171
  118.4 1.7 copy.169
  120.1 1.6 bitcast_negate_fusion.13
  121.7 1.7 copy.167
  123.3 1.6 bitcast_negate_fusion.14
  124.9 1.7 copy.165
  126.5 1.6 bitcast_negate_fusion.15
  129.2 2.0 fusion.158
  131.2 2.6 fusion.83
  133.7 2.5 fusion.75
  137.0 1.7 copy.192
  144.8 1.7 copy.172
  146.4 1.7 copy.170
  148.1 1.7 copy.168
  149.7 1.7 copy.166
  151.4 1.7 copy.164
  154.0 1.4 compare_reduce_fusion.7
  156.5 1.0 constant_dynamic-update-slice_fusion.5
  157.5 4.4 %collective-permute-start.3 = (bf16[6,1,32,512]{3,2,1,0:T(8,128)(2,1)S(1)}, bf16[6,1,32,512]{3,2,1,0:T(8,128)(2,1)S(1)}, u32[]{:S(2)}, u32[]{:S(2)}) collective-permute-start(bf16[6,1,32,512]{3,2,1,0:T(8,128)(2,1)S(1)} %get-tuple-element.82), channel_id=1, source_target_pairs={{1,0},{2,1},{3,2},{0,3},{5,4},{6,5},{7,6},{4,7},{9,8},{10,9},{11,1... | collective-permute-start | bytes 589832 | tf_op jit(solution)/shard_map/ppermute | solution.py:24
  161.9 2.4 convolution_select_fusion
  164.4 2.5 convolution_select_fusion.1
  167.9 1.5 convolution_select_fusion.4
  169.4 1.4 convolution_select_fusion.5
  171.6 1.5 convolution_select_fusion.6
  173.2 1.5 convolution_select_fusion.7
  174.7 1.4 convolution_select_fusion.8
  180.1 36.6 %reduce-scatter.4.cloned.1.call-done = f32[64,64]{1,0:T(8,128)} async-done(((f32[2048,64]{1,0:T(8,128)}), f32[64,64]{1,0:T(8,128)}) %reduce-scatter.4.cloned.1.call-update) | async-done | bytes 16400
  217.7 74.0 %all_gather.3 = bf16[32,2,2048]{0,1,2:T(2,128)(2,1)S(1)} all-gather(bf16[32,2,64]{0,1,2:T(2,128)(2,1)S(1)} %copy.112), channel_id=1, replica_groups=mesh['row'=8,'col'=4] {'row','col'}, dimensions={2}, use_global_device_ids=true | all-gather | bytes 270336 | tf_op jit(solution)/shard_map/all_gather | solution.py:101
  291.7 2.4 slice_convert_fusion.1
  294.2 1.5 copy.114
  295.7 2.3 copy.113
  298.0 2.4 add_convert_fusion
  300.5 2.4 fusion
  303.6 1.7 fusion.25
  (186 shorter events, 25.3 us)
Async XLA Ops:
  6.5 210.1 %reduce-scatter.4.cloned.1.call-start = ((), (), s32[]{:S(2)}) async-start(), calls=%async_computation.1 | async-start | bytes 1081344
  50.6 12.9 %copy-start.60 = (s32[4,4,2]{1,2,0:T(2,128)S(1)}, s32[4,4,2]{1,2,0:T(2,128)}, u32[]{:S(2)}) copy-start(s32[4,4,2]{1,2,0:T(2,128)} %param.10) | copy-start | bytes 388
  50.6 13.7 %copy-start.59 = (s32[2048,2]{0,1:T(2,128)S(1)}, s32[2048,2]{0,1:T(2,128)}, u32[]{:S(2)}) copy-start(s32[2048,2]{0,1:T(2,128)} %param.11) | copy-start | bytes 49156
  64.2 7.8 %copy-start.62 = (s32[4]{0:T(128)}, s32[4]{0:T(128)S(1)}, u32[]{:S(2)}) copy-start(s32[4]{0:T(128)S(1)} %add_multiply_fusion) | copy-start | bytes 52
  79.4 76.0 %collective-permute-start = (bf16[1,4,32,512]{3,2,1,0:T(8,128)(2,1)}, bf16[1,4,32,512]{3,2,1,0:T(8,128)(2,1)}, u32[]{:S(2)}, u32[]{:S(2)}) collective-permute-start(bf16[1,4,32,512]{3,2,1,0:T(8,128)(2,1)} %get-tuple-element.89), channel_id=1, source_target_pairs={{0,4},{4,8},{8,12},{12,16},{16,20},{20,24},{24,28},{28,0},{1,5},{5... | collective-permute-start | bytes 393224 | tf_op jit(solution)/shard_map/ppermute | solution.py:22
  79.8 76.7 %collective-permute-start.1 = (bf16[1,4,32,512]{3,2,1,0:T(8,128)(2,1)}, bf16[1,4,32,512]{3,2,1,0:T(8,128)(2,1)}, u32[]{:S(2)}, u32[]{:S(2)}) collective-permute-start(bf16[1,4,32,512]{3,2,1,0:T(8,128)(2,1)} %get-tuple-element.88), channel_id=1, source_target_pairs={{4,0},{8,4},{12,8},{16,12},{20,16},{24,20},{28,24},{0,28},{5,1},{9... | collective-permute-start | bytes 393224 | tf_op jit(solution)/shard_map/ppermute | solution.py:24
  90.8 40.3 %copy-start = (bf16[4,4,32,512]{3,2,1,0:T(8,128)(2,1)S(1)}, bf16[4,4,32,512]{3,2,1,0:T(8,128)(2,1)}, u32[]{:S(2)}) copy-start(bf16[4,4,32,512]{3,2,1,0:T(8,128)(2,1)} %param.7) | copy-start | bytes 1572868
  114.3 13.8 %copy-start.20 = (bf16[1,1,1,256,256]{3,4,2,1,0:T(8,128)(2,1)}, bf16[1,1,1,256,256]{3,4,2,1,0:T(8,128)(2,1)S(1)}, u32[]{:S(2)}) copy-start(bf16[1,1,1,256,256]{3,4,2,1,0:T(8,128)(2,1)S(1)} %copy.175) | copy-start | bytes 393220
  117.7 10.4 %copy-start.16 = (bf16[1,1,1,256,256]{3,4,2,1,0:T(8,128)(2,1)}, bf16[1,1,1,256,256]{3,4,2,1,0:T(8,128)(2,1)S(1)}, u32[]{:S(2)}) copy-start(bf16[1,1,1,256,256]{3,4,2,1,0:T(8,128)(2,1)S(1)} %copy.171) | copy-start | bytes 393220
  133.7 20.2 %copy-start.13 = (s32[4,4,9]{2,1,0:T(4,128)S(1)}, s32[4,4,9]{2,1,0:T(4,128)}, u32[]{:S(2)}) copy-start(s32[4,4,9]{2,1,0:T(4,128)} %param.9) | copy-start | bytes 1732
  143.2 18.7 %copy-start.56 = (bf16[1,1,1,256,256]{3,4,2,1,0:T(8,128)(2,1)S(1)}, bf16[1,1,1,256,256]{3,4,2,1,0:T(8,128)(2,1)}, u32[]{:S(2)}) copy-start(bf16[1,1,1,256,256]{3,4,2,1,0:T(8,128)(2,1)} %copy.188) | copy-start | bytes 393220
  149.7 14.6 %copy-start.29 = (bf16[1,1,1,256,256]{3,4,2,1,0:T(8,128)(2,1)S(1)}, bf16[1,1,1,256,256]{3,4,2,1,0:T(8,128)(2,1)}, u32[]{:S(2)}) copy-start(bf16[1,1,1,256,256]{3,4,2,1,0:T(8,128)(2,1)} %copy.187) | copy-start | bytes 393220
  156.5 10.4 %copy-start.31 = (bf16[1,1,1,256,256]{3,4,2,1,0:T(8,128)(2,1)S(1)}, bf16[1,1,1,256,256]{3,4,2,1,0:T(8,128)(2,1)}, u32[]{:S(2)}) copy-start(bf16[1,1,1,256,256]{3,4,2,1,0:T(8,128)(2,1)} %copy.169) | copy-start | bytes 393220
  156.5 10.4 %copy-start.45 = (bf16[256,256]{1,0:T(8,128)(2,1)S(1)}, bf16[256,256]{1,0:T(8,128)(2,1)}, u32[]{:S(2)}) copy-start(bf16[256,256]{1,0:T(8,128)(2,1)} %bitcast_negate_fusion.13) | copy-start | bytes 393220
  156.5 10.4 %copy-start.58 = (bf16[1,1,1,256,256]{3,4,2,1,0:T(8,128)(2,1)S(1)}, bf16[1,1,1,256,256]{3,4,2,1,0:T(8,128)(2,1)}, u32[]{:S(2)}) copy-start(bf16[1,1,1,256,256]{3,4,2,1,0:T(8,128)(2,1)} %copy.168) | copy-start | bytes 393220
  157.5 10.4 %collective-permute-start.3 = (bf16[6,1,32,512]{3,2,1,0:T(8,128)(2,1)S(1)}, bf16[6,1,32,512]{3,2,1,0:T(8,128)(2,1)S(1)}, u32[]{:S(2)}, u32[]{:S(2)}) collective-permute-start(bf16[6,1,32,512]{3,2,1,0:T(8,128)(2,1)S(1)} %get-tuple-element.82), channel_id=1, source_target_pairs={{1,0},{2,1},{3,2},{0,3},{5,4},{6,5},{7,6},{4,7},{9,8},{10,9},{11,1... | collective-permute-start | bytes 589832 | tf_op jit(solution)/shard_map/ppermute | solution.py:24
  161.9 9.7 %collective-permute-start.2 = (bf16[6,1,32,512]{3,2,1,0:T(8,128)(2,1)S(1)}, bf16[6,1,32,512]{3,2,1,0:T(8,128)(2,1)S(1)}, u32[]{:S(2)}, u32[]{:S(2)}) collective-permute-start(bf16[6,1,32,512]{3,2,1,0:T(8,128)(2,1)S(1)} %get-tuple-element.81), channel_id=1, source_target_pairs={{0,1},{1,2},{2,3},{3,0},{4,5},{5,6},{6,7},{7,4},{8,9},{9,10},{10,1... | collective-permute-start | bytes 589832 | tf_op jit(solution)/shard_map/ppermute | solution.py:22
  164.3 3.0 copy-start.30
  164.4 3.0 copy-start.44
  164.4 3.1 copy-start.57
  166.9 1.0 copy-start.28
  166.9 1.0 copy-start.43
  166.9 1.0 copy-start.55
  167.4 2.0 copy-start.26
  167.4 2.0 copy-start.41
  167.4 2.0 copy-start.54
  167.9 9.7 %copy-start.32 = (bf16[6,1,32,512]{3,2,1,0:T(8,128)(2,1)}, bf16[6,1,32,512]{3,2,1,0:T(8,128)(2,1)S(1)}, u32[]{:S(2)}) copy-start(bf16[6,1,32,512]{3,2,1,0:T(8,128)(2,1)S(1)} %collective-permute-done.3) | copy-start | bytes 589828
  167.9 3.7 %copy-start.27 = (bf16[1,1,1,256,256]{3,4,2,1,0:T(8,128)(2,1)S(1)}, bf16[1,1,1,256,256]{3,4,2,1,0:T(8,128)(2,1)}, u32[]{:S(2)}) copy-start(bf16[1,1,1,256,256]{3,4,2,1,0:T(8,128)(2,1)} %copy.185) | copy-start | bytes 393220
  167.9 3.7 %copy-start.42 = (bf16[256,256]{1,0:T(8,128)(2,1)S(1)}, bf16[256,256]{1,0:T(8,128)(2,1)}, u32[]{:S(2)}) copy-start(bf16[256,256]{1,0:T(8,128)(2,1)} %bitcast_negate_fusion.5) | copy-start | bytes 393220
  167.9 3.7 %copy-start.53 = (bf16[1,1,1,256,256]{3,4,2,1,0:T(8,128)(2,1)S(1)}, bf16[1,1,1,256,256]{3,4,2,1,0:T(8,128)(2,1)}, u32[]{:S(2)}) copy-start(bf16[1,1,1,256,256]{3,4,2,1,0:T(8,128)(2,1)} %copy.184) | copy-start | bytes 393220
  169.4 3.7 %copy-start.25 = (bf16[1,1,1,256,256]{3,4,2,1,0:T(8,128)(2,1)S(1)}, bf16[1,1,1,256,256]{3,4,2,1,0:T(8,128)(2,1)}, u32[]{:S(2)}) copy-start(bf16[1,1,1,256,256]{3,4,2,1,0:T(8,128)(2,1)} %copy.183) | copy-start | bytes 393220
  169.4 3.7 %copy-start.40 = (bf16[256,256]{1,0:T(8,128)(2,1)S(1)}, bf16[256,256]{1,0:T(8,128)(2,1)}, u32[]{:S(2)}) copy-start(bf16[256,256]{1,0:T(8,128)(2,1)} %bitcast_negate_fusion.6) | copy-start | bytes 393220
  169.4 3.7 %copy-start.52 = (bf16[1,1,1,256,256]{3,4,2,1,0:T(8,128)(2,1)S(1)}, bf16[1,1,1,256,256]{3,4,2,1,0:T(8,128)(2,1)}, u32[]{:S(2)}) copy-start(bf16[1,1,1,256,256]{3,4,2,1,0:T(8,128)(2,1)} %copy.182) | copy-start | bytes 393220
  171.6 3.1 copy-start.24
  171.6 3.1 copy-start.39
  171.6 3.0 copy-start.51
  173.1 3.0 copy-start.23
  173.1 3.0 copy-start.38
  173.1 3.0 copy-start.50
  174.7 1.9 copy-start.21
  174.7 1.9 copy-start.36
  174.7 1.9 copy-start.49
  176.1 1.0 copy-start.19
  176.1 1.0 copy-start.35
  176.1 1.0 copy-start.48
  176.6 1.0 copy-start.17
  176.6 1.0 copy-start.34
  176.7 1.0 copy-start.46
  177.2 1.0 copy-start.37
  177.2 1.0 copy-start.47
  177.7 1.3 copy-start.2
  177.7 1.6 copy-start.3
  180.1 117.9 %copy-start.15 = (f32[4,4,2048]{2,1,0:T(4,128)S(1)}, f32[4,4,2048]{2,1,0:T(4,128)}, u32[]{:S(2)}) copy-start(f32[4,4,2048]{2,1,0:T(4,128)} %get-tuple-element.94) | copy-start | bytes 393220
  298.0 2.4 copy-start.1
  298.0 2.4 copy-start.12
  300.4 2.5 copy-start.4
  300.4 2.5 copy-start.5
  300.4 2.5 copy-start.6
  300.4 2.5 copy-start.7
  300.5 2.5 copy-start.8
  300.5 2.8 copy-start.9
  300.5 3.1 copy-start.10
  300.5 3.1 copy-start.14
  300.5 3.1 copy-start.33
  (4 other events, 3.2 us)
Sparse Core Ops, SparseCore 0:
  77.8 138.8 reduce-scatter.3
where the time goes:
time: 314 us; the launch traced here: 312 us
  local copies, waits for them, and re-layouts  107 us (34%)
  blocking collectives  74 us (24%)
  other arithmetic  39.5 us (13%)
  waiting for transfers between devices  37.3 us (12%)
  matrix products  32.6 us (10%)
  between operations  14.2 us (5%)
  starting transfers between devices  7.75 us (2%)
    all_gather x1, blocking collectives, local(): add_weighted = lax.all_gather(weighted, ('row', 'col'), axis=2, tiled=True)  74 us
    unnamed x165, local copies, waits for them, and re-layouts  53.8 us
    unnamed x2, waiting for transfers between devices  36.6 us
    dot_general x18, matrix products, local(): jnp.dot(block, near_mat, preferred_element_type=jnp.float32)  22.9 us
    neg x18, other arithmetic, realify(): lower = jnp.concatenate([-imag_part.T, real_part.T], axis=1)  21.2 us
    slice x1, local copies, waits for them, and re-layouts, local(): projected[:, :, 1]  12.2 us
    reshape x1, local copies, waits for them, and re-layouts, local(): projected = projected.reshape(rows_here * cols_here, sources, 2, waves)  11.8 us
    dot_general x1, local copies, waits for them, and re-layouts, local(): jnp.dot(field.reshape(-1, width), wave_matrix, preferred_element_type=jnp...  8.97 us
  transfers between devices with their start and end apart: 5, of which 2 were waited for; matrix products, arithmetic and copies ran while one was open for 30% of the time, Pallas kernels for 0%

commit v1 on v0

v1 whole, which is shorter than its diff:
```python
import math

import jax
import jax.numpy as jnp
from jax import lax
from jax.experimental import pallas as pl
from jax.experimental.pallas import tpu as pltpu
from jax.sharding import PartitionSpec as P

Q = 16
LANES = 128

bloch_row = 0.3
bloch_col = 0.17

F32 = jnp.float32
BF16 = jnp.bfloat16
NT = (((1,), (1,)), ((), ()))
HBM = pl.BlockSpec(memory_space=pltpu.MemorySpace.HBM)
VMEM = pl.BlockSpec(memory_space=pltpu.MemorySpace.VMEM)
SMEM = pl.BlockSpec(memory_space=pltpu.MemorySpace.SMEM)


def params(mib):
    return pltpu.CompilerParams(vmem_limit_bytes=mib << 20)


def cost(flops, size):
    return pl.CostEstimate(flops=flops, bytes_accessed=size, transcendentals=0)


def unit(turn):
    y = math.pi * turn
    z = y * y
    even = [(-1) ** k / math.factorial(2 * k) for k in range(8)]
    odd = [(-1) ** k / math.factorial(2 * k + 1) for k in range(8)]
    c = even[7]
    s = odd[7]
    for k in range(6, -1, -1):
        c = c * z + even[k]
        s = s * z + odd[k]
    s = s * y
    return 1.0 - 2.0 * (s * s), 2.0 * (s * c)


def fine(shift, lanes):
    rows, cols = shift.shape[0], shift.shape[2]
    first_row = lax.axis_index("row") * rows
    first_col = lax.axis_index("col") * cols
    spot = lax.broadcasted_iota(jnp.int32, (rows * cols, lanes), 0)
    fr = jnp.zeros(spot.shape, jnp.int32)
    fc = fr
    for p in range(rows * cols):
        r, c = p // cols, p % cols
        fr = jnp.where(spot == p, Q * (first_row + r) + shift[r, 0, c], fr)
        fc = jnp.where(spot == p, Q * (first_col + c) + shift[r, 1, c], fc)
    return fr, fc


def phases(fr, fc, index, row_mod, col_mod):
    turn_row = ((index[0:1] * fr) & (row_mod - 1)).astype(F32) * (1.0 / row_mod)
    turn_col = ((index[1:2] * fc) & (col_mod - 1)).astype(F32) * (1.0 / col_mod)
    drift = (bloch_row / row_mod) * fr.astype(F32) + (bloch_col / col_mod) * fc.astype(F32)
    turn = turn_row + turn_col + drift
    return unit(turn - jnp.round(turn))


def project_body(x_hbm, shift_hbm, index_hbm, weight_hbm, wave_hbm, mine_ref, other_ref, form_ref,
                 xs, left, right, shift, index_ref, weight_ref, g, sem, gsem,
                 *, tile, row_mod, col_mod, scale):
    waves = wave_hbm.shape[0]
    half = waves // 2
    width = wave_hbm.shape[2]
    n = shift.shape[0] * shift.shape[2]
    sources = x_hbm.shape[0] // n
    core = lax.axis_index("row") & 1
    small = [
        pltpu.make_async_copy(src, dst, sem.at[k])
        for k, (src, dst) in enumerate(
            ((x_hbm, xs), (shift_hbm, shift), (index_hbm, index_ref), (weight_hbm, weight_ref))
        )
    ]
    for c in small:
        c.start()
    steps = []
    for t in range(waves // tile):
        flip = 1 if t < waves // tile // 2 else 0
        inside = (t * tile) % half
        first = pl.multiple_of((core ^ flip) * half + inside, tile)
        pair = [
            pltpu.make_async_copy(
                wave_hbm.at[pl.ds(first, tile), :, pl.ds(LANES * j, LANES)], g.at[j, t], gsem.at[t, j]
            )
            for j in range(2)
        ]
        for c in pair:
            c.start()
        steps.append((flip, inside, first, pair))
    a = lax.broadcasted_iota(jnp.int32, (2 * LANES, 2 * LANES), 0)
    b = lax.broadcasted_iota(jnp.int32, (2 * LANES, 2 * LANES), 1)
    sort = jnp.where(b == jnp.where(a < LANES, 2 * a, 2 * (a - LANES) + 1), 1.0, 0.0).astype(BF16)
    for c in small:
        c.wait()
    left[:, :width] = xs[:, :width]
    left[:, width:] = -xs[:, width:]
    right[:, :width] = xs[:, width:]
    right[:, width:] = xs[:, :width]
    fr, fc = fine(shift, tile)
    for t, (flip, inside, first, pair) in enumerate(steps):
        for c in pair:
            c.wait()
        for k in range(tile // LANES):
            at = pl.ds(first + k * LANES, LANES)
            mixed = jnp.concatenate(
                [g[j, t, k * LANES : (k + 1) * LANES].reshape(2 * LANES, LANES) for j in range(2)], axis=1
            )
            d = jnp.dot(sort, mixed, preferred_element_type=F32).astype(BF16)
            form_ref[0, at, :] = d[:LANES]
            form_ref[1, at, :] = d[LANES:]
        at = pl.ds(first, tile)
        w = jnp.concatenate([form_ref[0, at, :], form_ref[1, at, :]], axis=1)
        re = lax.dot_general(left[...], w, NT, preferred_element_type=F32)
        im = lax.dot_general(right[...], w, NT, preferred_element_type=F32)
        cos, sin = phases(fr, fc, index_ref[:, at], row_mod, col_mod)
        ar = jnp.zeros((sources, tile), F32)
        ai = ar
        for p in range(n):
            u = re[p * sources : (p + 1) * sources]
            v = im[p * sources : (p + 1) * sources]
            cp, sp = cos[p : p + 1], sin[p : p + 1]
            ar = ar + (cp * u - sp * v)
            ai = ai + (cp * v + sp * u)
        s = scale * weight_ref[:, at]
        ar = ar * s
        ai = ai * s
        out = other_ref if flip else mine_ref
        for k in range(tile // LANES):
            out[inside // LANES + k, 0] = ar[:, LANES * k : LANES * (k + 1)]
            out[inside // LANES + k, 1] = ai[:, LANES * k : LANES * (k + 1)]


def project(x, shift, index, weight, wave_form, row_mod, col_mod, scale, tile=512):
    waves, _, width = wave_form.shape
    n = shift.shape[0] * shift.shape[2]
    sources = x.shape[0] // n
    half = jax.ShapeDtypeStruct((waves // 2 // LANES, 2, sources, LANES), F32)

    def body(*refs):
        project_body(*refs, tile=tile, row_mod=row_mod, col_mod=col_mod, scale=scale)

    return pl.pallas_call(
        body,
        in_specs=[HBM] * 5,
        out_specs=[VMEM] * 3,
        out_shape=[half, half, jax.ShapeDtypeStruct((2, waves, width), BF16)],
        scratch_shapes=[
            pltpu.VMEM(x.shape, BF16),
            pltpu.VMEM(x.shape, BF16),
            pltpu.VMEM(x.shape, BF16),
            pltpu.SMEM(shift.shape, jnp.int32),
            pltpu.VMEM(index.shape, jnp.int32),
            pltpu.VMEM(weight.shape, F32),
            pltpu.VMEM((2, waves // tile, tile, 2, LANES), BF16),
            pltpu.SemaphoreType.DMA((4,)),
            pltpu.SemaphoreType.DMA((waves // tile, 2)),
        ],
        compiler_params=params(24),
        cost_estimate=cost(8 * x.shape[0] * width * waves, 5 << 20),
        name="project",
    )(x, shift, index, weight, wave_form)


def spread_body(shift_hbm, index_hbm, form_hbm, coeff_ref, base_ref, out_ref, shift, index_ref, form_ref,
                lhs, sem, *, flip, tile, row_mod, col_mod):
    half = form_ref.shape[1]
    width = form_ref.shape[2]
    n = shift.shape[0] * shift.shape[2]
    sources = coeff_ref.shape[2]
    core = (lax.axis_index("row") & 1) ^ flip
    start = pl.multiple_of(core * half, half)
    copies = [
        pltpu.make_async_copy(shift_hbm, shift, sem.at[0]),
        pltpu.make_async_copy(index_hbm.at[:, pl.ds(start, half)], index_ref, sem.at[1]),
        pltpu.make_async_copy(form_hbm.at[:, pl.ds(start, half)], form_ref, sem.at[2]),
    ]
    for c in copies:
        c.start()
    copies[0].wait()
    copies[1].wait()
    fr, fc = fine(shift, tile)
    for t in range(half // tile):
        at = slice(t * tile, (t + 1) * tile)
        cos, sin = phases(fr, fc, index_ref[:, at], row_mod, col_mod)
        groups = range(t * tile // LANES, (t + 1) * tile // LANES)
        wr = jnp.concatenate([coeff_ref[k, 0].astype(F32) for k in groups], axis=1)
        wi = jnp.concatenate([coeff_ref[k, 1].astype(F32) for k in groups], axis=1)
        for p in range(n):
            cp, sp = cos[p : p + 1], sin[p : p + 1]
            sr = (cp * wr + sp * wi).astype(BF16)
            si = (cp * wi - sp * wr).astype(BF16)
            here = slice(p * sources, (p + 1) * sources)
            lhs[0, here, :tile] = sr
            lhs[0, here, tile:] = si
            lhs[1, here, :tile] = si
            lhs[1, here, tile:] = -sr
        if t == 0:
            copies[2].wait()
        w = jnp.concatenate([form_ref[0, at, :], form_ref[1, at, :]], axis=0)
        src = base_ref if t == 0 else out_ref
        for j in range(2):
            cols = slice(j * width, (j + 1) * width)
            out_ref[:, cols] = src[:, cols] + jnp.dot(lhs[j], w, preferred_element_type=F32)


def spread(shift, index, form, coeff, base, row_mod, col_mod, flip, tile=256):
    waves, width = form.shape[1], form.shape[2]

    def body(*refs):
        spread_body(*refs, flip=flip, tile=tile, row_mod=row_mod, col_mod=col_mod)

    return pl.pallas_call(
        body,
        in_specs=[HBM, HBM, HBM, VMEM, VMEM],
        out_specs=VMEM,
        out_shape=jax.ShapeDtypeStruct(base.shape, F32),
        scratch_shapes=[
            pltpu.SMEM(shift.shape, jnp.int32),
            pltpu.VMEM((2, waves // 2), jnp.int32),
            pltpu.VMEM((2, waves // 2, width), BF16),
            pltpu.VMEM((2, base.shape[0], 2 * tile), BF16),
            pltpu.SemaphoreType.DMA((3,)),
        ],
        compiler_params=params(24),
        cost_estimate=cost(2 * base.shape[0] * base.shape[1] * waves, 5 << 20),
        name="spread",
    )(shift, index, form, coeff, base)


def near_body(contact_hbm, x_hbm, north_hbm, south_hbm, west_hbm, east_hbm, kernel_hbm, out_ref,
              contact, x, north, south, west, east, kernel, lhs, sem, ksem):
    rows, cols, sources, full = x.shape
    width = full // 2
    offsets, classes = kernel.shape[0], kernel.shape[1]
    small = [
        pltpu.make_async_copy(src, dst, sem.at[k])
        for k, (src, dst) in enumerate(
            ((contact_hbm, contact), (x_hbm, x), (north_hbm, north), (south_hbm, south),
             (west_hbm, west), (east_hbm, east))
        )
    ]
    for c in small:
        c.start()
    big = [pltpu.make_async_copy(kernel_hbm.at[o], kernel.at[o], ksem.at[o]) for o in range(offsets)]
    for c in big:
        c.start()
    for c in small:
        c.wait()

    def block(r, c):
        if r < 0:
            return north[0, c + 1]
        if r >= rows:
            return south[0, c + 1]
        if c < 0:
            return west[r, 0]
        if c >= cols:
            return east[r, 0]
        return x[r, c]

    for o in range(offsets):
        for p in range(rows * cols):
            r, c = p // cols, p % cols
            here = slice(p * sources, (p + 1) * sources)
            xb = block(r + o // 3 - 1, c + o % 3 - 1)
            for v in range(classes):
                m = jnp.where(contact[r, c, o] == v, xb, jnp.zeros_like(xb))
                lhs[v, here, :full] = m
                lhs[v, here, full:] = -m[:, width:]
        big[o].wait()
        for v in range(classes):
            xr, xi, nx = (lhs[v, :, k * width : (k + 1) * width] for k in range(3))
            w = jnp.concatenate([kernel[o, v, 0], kernel[o, v, 1]], axis=1)
            re = lax.dot_general(jnp.concatenate([xr, nx], axis=1), w, NT, preferred_element_type=F32)
            im = lax.dot_general(jnp.concatenate([xi, xr], axis=1), w, NT, preferred_element_type=F32)
            if o == 0 and v == 0:
                out_ref[:, :width] = re
                out_ref[:, width:] = im
            else:
                out_ref[:, :width] += re
                out_ref[:, width:] += im


def near_field(contact, x, north, south, west, east, kernel):
    rows, cols, sources, full = x.shape
    m = rows * cols * sources
    return pl.pallas_call(
        near_body,
        in_specs=[HBM] * 7,
        out_specs=VMEM,
        out_shape=jax.ShapeDtypeStruct((m, full), F32),
        scratch_shapes=[pltpu.SMEM(contact.shape, jnp.int32)]
        + [pltpu.VMEM(a.shape, BF16) for a in (x, north, south, west, east, kernel)]
        + [
            pltpu.VMEM((kernel.shape[1], m, 3 * full // 2), BF16),
            pltpu.SemaphoreType.DMA((6,)),
            pltpu.SemaphoreType.DMA((kernel.shape[0],)),
        ],
        compiler_params=params(32),
        cost_estimate=cost(2 * kernel.shape[0] * kernel.shape[1] * m * full * full, 8 << 20),
        name="near",
    )(contact, x, north, south, west, east, kernel)


def shifted(cells, axis, step):
    count = lax.axis_size(axis)
    return lax.ppermute(cells, axis, [(i, (i + step) % count) for i in range(count)])


def bits(count, first):
    out = []
    while first < count:
        out.append(first)
        first *= 2
    return out


def exchange(value, dims):
    n_row, n_col = lax.axis_size("row"), lax.axis_size("col")
    pairs = []
    for r in range(n_row):
        for c in range(n_col):
            dr, dc = dims[r & 1]
            pairs.append((r * n_col + c, (r ^ dr) * n_col + (c ^ dc)))
    return lax.ppermute(value, ("row", "col"), pairs)


def local(field, near_kernel, contact, pillar_shift, wave_index, wave_form, wave_weight):
    rows, cols, sources, full = field.shape
    waves = wave_form.shape[0]
    n_row, n_col = lax.axis_size("row"), lax.axis_size("col")
    row_mod = Q * rows * n_row
    col_mod = Q * cols * n_col
    scale = math.sqrt(full // 2 / (waves * rows * n_row * cols * n_col))
    shift = jnp.swapaxes(pillar_shift, 1, 2)
    index = wave_index.T
    weight = wave_weight.reshape(1, -1)
    mine, other, form = project(
        field.reshape(-1, full), shift, index, weight, wave_form, row_mod, col_mod, scale
    )
    total = mine + exchange(other, ((1, 0), (1, 0)))
    by_row = [(b, 0) for b in bits(n_row, 2)]
    by_col = [(0, b) for b in bits(n_col, 1)]
    for dims in zip(by_row + by_col, by_row[::-1] + by_col):
        total = total + exchange(total.astype(jnp.float16), dims).astype(F32)
    weighted = total.astype(BF16)
    weighted_other = exchange(weighted, ((1, 0), (1, 0)))
    west = shifted(field[:, cols - 1 :], "col", 1)
    east = shifted(field[:, :1], "col", -1)
    wide_top = jnp.concatenate([west[:1], field[:1], east[:1]], axis=1)
    wide_bottom = jnp.concatenate([west[-1:], field[-1:], east[-1:]], axis=1)
    north = shifted(wide_bottom, "row", 1)
    south = shifted(wide_top, "row", -1)
    out = near_field(contact, field, north, south, west, east, near_kernel)
    out = spread(shift, index, form, weighted, out, row_mod, col_mod, 0)
    out = spread(shift, index, form, weighted_other, out, row_mod, col_mod, 1)
    return out.reshape(field.shape)


def solution(mesh):
    placed = (
        P("row", "col", None, None),
        P(),
        P("row", "col", None),
        P("row", "col", None),
        P(),
        P(),
        P(),
    )
    return jax.shard_map(
        local, mesh=mesh, in_specs=placed, out_specs=P("row", "col", None, None), check_vma=False
    )
```

time: 314 us -> 54 us (0.17)
  the two profiles are of different devices: /device:TPU:0 before, /device:TPU:1 now
where the time goes in v1:
time: 54 us; the launch traced here: 53.7 us
  Pallas kernels  19.5 us (36%)
  starting transfers between devices  17.9 us (33%)
  waiting for transfers between devices  10.8 us (20%)
  local copies, waits for them, and re-layouts  4.81 us (9%)
    ppermute x4, starting transfers between devices, shifted(): lax.ppermute(cells, axis, [(i, (i + step) % count) for i in range(count)])  10.3 us
    ppermute x6, waiting for transfers between devices, exchange(): return lax.ppermute(value, ('row', 'col'), pairs)  9.21 us
    pallas_call x1, Pallas kernels, near_field(): pl.pallas_call(near_body, in_specs=[HBM] * 7, out_specs=VMEM, out_shape=j...  7.65 us
    ppermute x6, starting transfers between devices, exchange(): return lax.ppermute(value, ('row', 'col'), pairs)  7.59 us
    pallas_call x1, Pallas kernels, project(): pl.pallas_call(body, in_specs=[HBM] * 5, out_specs=[VMEM] * 3, out_shape=...  6.77 us
    pallas_call x2, Pallas kernels, spread(): pl.pallas_call(body, in_specs=[HBM, HBM, HBM, VMEM, VMEM], out_specs=VMEM...  5.06 us
    unnamed x20, local copies, waits for them, and re-layouts  4.76 us
    ppermute x4, waiting for transfers between devices, shifted(): lax.ppermute(cells, axis, [(i, (i + step) % count) for i in range(count)])  1.59 us
  transfers between devices with their start and end apart: 10, of which 4 were waited for; matrix products, arithmetic and copies ran while one was open for 1% of the time, Pallas kernels for 18%

profile of v1, /device:TPU:1, one launch (start us, length us, event | category | flops | bytes accessed | tf_op | source)
XLA Modules:
  0.0 53.7 jit_solution(5173599653892045031)
XLA Ops:
  0.0 0.0 copy-start
  0.0 1.0 %copy-done = bf16[4,4,32,512]{3,2,1,0:T(8,128)(2,1)S(1)} copy-done((bf16[4,4,32,512]{3,2,1,0:T(8,128)(2,1)S(1)}, bf16[4,4,32,512]{3,2,1,0:T(8,128)(2,1)}, u32[]{:S(2)}) %copy-start) | copy-done | bytes 524312
  1.0 0.0 copy-start.2
  1.0 0.7 %copy-done.2 = s32[2048,2]{0,1:T(2,128)S(1)} copy-done((s32[2048,2]{0,1:T(2,128)S(1)}, s32[2048,2]{0,1:T(2,128)}, u32[]{:S(2)}) %copy-start.2) | copy-done | bytes 16408
  1.8 0.0 copy-start.4
  1.8 0.7 %copy-done.4 = s32[4,4,2]{1,2,0:T(2,128)S(1)} copy-done((s32[4,4,2]{1,2,0:T(2,128)S(1)}, s32[4,4,2]{1,2,0:T(2,128)}, u32[]{:S(2)}) %copy-start.4) | copy-done | bytes 152
  2.4 0.0 copy-start.7
  2.5 1.6 %copy-done.7 = bf16[2048,2,256]{2,1,0:T(2,128)(2,1)S(1)} copy-done((bf16[2048,2,256]{2,1,0:T(2,128)(2,1)S(1)}, bf16[2048,2,256]{2,1,0:T(2,128)(2,1)}, u32[]{:S(2)}) %copy-start.7) | copy-done | bytes 2097176
  4.0 0.0 copy-start.8
  4.0 0.7 %copy-done.8 = f32[2048]{0:T(1024)S(1)} copy-done((f32[2048]{0:T(1024)S(1)}, f32[2048]{0:T(1024)}, u32[]{:S(2)}) %copy-start.8) | copy-done | bytes 8216
  4.7 6.8 %project.1 = (f32[8,2,32,128]{3,2,1,0:T(8,128)S(1)}, f32[8,2,32,128]{3,2,1,0:T(8,128)S(1)}, bf16[2,2048,256]{2,1,0:T(8,128)(2,1)S(1)}) custom-call(bf16[512,512]{1,0:T(8,128)(2,1)S(1)} %bitcast.5, s32[4,2,4]{2,1,0:T(2,128)S(1)} %bitcast.9, s32[2,2048]{1,0:T(2,128)S(1)} %bitcast.6, f32[1,2048]{1,0:T(1,128)S(1)} %bitcast.12, bf16[2048,2,256]{2,1,0:T(2,128)(2,1)S(1)} %copy-done.7), custom_call_target="tpu_custom_call" | custom-call | flops 2147483648 | bytes 5242880 | tf_op jit(solution)/shard_map/project/pallas_call | solution.py:151
  11.5 0.1 collective-permute-start
  11.7 2.8 %collective-permute-start.6 = (bf16[4,1,32,512]{3,2,1,0:T(8,128)(2,1)S(1)}, bf16[4,1,32,512]{3,2,1,0:T(8,128)(2,1)S(1)}, u32[]{:S(2)}, u32[]{:S(2)}) collective-permute-start(bf16[4,1,32,512]{3,2,1,0:T(8,128)(2,1)S(1)} %get-tuple-element.15), channel_id=1, source_target_pairs={{0,1},{1,2},{2,3},{3,0},{4,5},{5,6},{6,7},{7,4},{8,9},{9,10},{10,1... | collective-permute-start | bytes 393224 | tf_op jit(solution)/shard_map/ppermute | solution.py:316
  14.5 2.1 %collective-permute-start.7 = (bf16[4,1,32,512]{3,2,1,0:T(8,128)(2,1)S(1)}, bf16[4,1,32,512]{3,2,1,0:T(8,128)(2,1)S(1)}, u32[]{:S(2)}, u32[]{:S(2)}) collective-permute-start(bf16[4,1,32,512]{3,2,1,0:T(8,128)(2,1)S(1)} %get-tuple-element.16), channel_id=1, source_target_pairs={{0,3},{1,0},{2,1},{3,2},{4,7},{5,4},{6,5},{7,6},{8,11},{9,8},{10,9... | collective-permute-start | bytes 393224 | tf_op jit(solution)/shard_map/ppermute | solution.py:316
  16.5 0.0 collective-permute-done
  16.5 0.0 copy-start.6
  16.6 1.3 %collective-permute-start.1 = (f16[8,2,32,128]{3,2,1,0:T(8,128)(2,1)S(1)}, f16[8,2,32,128]{3,2,1,0:T(8,128)(2,1)S(1)}, u32[]{:S(2)}, u32[]{:S(2)}) collective-permute-start(f16[8,2,32,128]{3,2,1,0:T(8,128)(2,1)S(1)} %get-tuple-element.11), channel_id=1, source_target_pairs={{0,8},{1,9},{2,10},{3,11},{4,20},{5,21},{6,22},{7,23},{8,0},{9,1},... | collective-permute-start | bytes 393224 | tf_op jit(solution)/shard_map/ppermute | solution.py:334
  17.9 0.0 copy-start.1
  17.9 0.0 copy-start.9
  18.0 2.8 %collective-permute-done.1 = f16[8,2,32,128]{3,2,1,0:T(8,128)(2,1)S(1)} collective-permute-done((f16[8,2,32,128]{3,2,1,0:T(8,128)(2,1)S(1)}, f16[8,2,32,128]{3,2,1,0:T(8,128)(2,1)S(1)}, u32[]{:S(2)}, u32[]{:S(2)}) %collective-permute-start.1) | collective-permute-done | bytes 131104 | tf_op jit(solution)/shard_map/ppermute | solution.py:334
  20.8 1.3 %collective-permute-start.2 = (f16[8,2,32,128]{3,2,1,0:T(8,128)(2,1)S(1)}, f16[8,2,32,128]{3,2,1,0:T(8,128)(2,1)S(1)}, u32[]{:S(2)}, u32[]{:S(2)}) collective-permute-start(f16[8,2,32,128]{3,2,1,0:T(8,128)(2,1)S(1)} %fusion), channel_id=1, source_target_pairs={{0,16},{1,17},{2,18},{3,19},{4,12},{5,13},{6,14},{7,15},{8,24},{9,... | collective-permute-start | bytes 393224 | tf_op jit(solution)/shard_map/ppermute | solution.py:334
  22.1 0.0 collective-permute-done.6.west_hbm
  22.1 2.6 %collective-permute-done.2 = f16[8,2,32,128]{3,2,1,0:T(8,128)(2,1)S(1)} collective-permute-done((f16[8,2,32,128]{3,2,1,0:T(8,128)(2,1)S(1)}, f16[8,2,32,128]{3,2,1,0:T(8,128)(2,1)S(1)}, u32[]{:S(2)}, u32[]{:S(2)}) %collective-permute-start.2) | collective-permute-done | bytes 131104 | tf_op jit(solution)/shard_map/ppermute | solution.py:334
  24.7 0.1 fusion.2
  24.8 0.1 collective-permute-start.3
  24.9 0.0 collective-permute-done.7.east_hbm
  24.9 3.8 %collective-permute-done.3 = f16[8,2,32,128]{3,2,1,0:T(8,128)(2,1)S(1)} collective-permute-done((f16[8,2,32,128]{3,2,1,0:T(8,128)(2,1)S(1)}, f16[8,2,32,128]{3,2,1,0:T(8,128)(2,1)S(1)}, u32[]{:S(2)}, u32[]{:S(2)}) %collective-permute-start.3) | collective-permute-done | bytes 131104 | tf_op jit(solution)/shard_map/ppermute | solution.py:334
  28.7 0.1 fusion.1
  28.8 0.5 collective-permute-start.4
  29.2 5.2 %collective-permute-start.8 = (bf16[1,6,32,512]{3,2,1,0:T(8,128)(2,1)S(1)}, bf16[1,6,32,512]{3,2,1,0:T(8,128)(2,1)S(1)}, u32[]{:S(2)}, u32[]{:S(2)}) collective-permute-start(bf16[1,6,32,512]{3,2,1,0:T(8,128)(2,1)S(1)} %pad_maximum_fusion), channel_id=1, source_target_pairs={{0,4},{4,8},{8,12},{12,16},{16,20},{20,24},{24,28},{28,0},{1,5},{5... | collective-permute-start | bytes 589832 | tf_op jit(solution)/shard_map/ppermute | solution.py:316
  34.4 0.2 collective-permute-start.9
  34.7 0.0 collective-permute-done.4
  34.7 0.1 add_convert_fusion.refs_3_
  34.8 0.0 copy-start.3
  34.8 0.0 copy-start.5
  34.8 4.4 %collective-permute-start.5 = (bf16[8,2,32,128]{3,2,1,0:T(8,128)(2,1)S(1)}, bf16[8,2,32,128]{3,2,1,0:T(8,128)(2,1)S(1)}, u32[]{:S(2)}, u32[]{:S(2)}) collective-permute-start(bf16[8,2,32,128]{3,2,1,0:T(8,128)(2,1)S(1)} %add_convert_fusion.refs_3_), channel_id=1, source_target_pairs={{0,4},{1,5},{2,6},{3,7},{4,0},{5,1},{6,2},{7,3},{8,12},{9,13},{10,... | collective-permute-start | bytes 393224 | tf_op jit(solution)/shard_map/ppermute | solution.py:334
  39.2 0.0 collective-permute-done.8.north_hbm
  39.2 1.6 %collective-permute-done.9.south_hbm = bf16[1,6,32,512]{3,2,1,0:T(8,128)(2,1)S(1)} collective-permute-done((bf16[1,6,32,512]{3,2,1,0:T(8,128)(2,1)S(1)}, bf16[1,6,32,512]{3,2,1,0:T(8,128)(2,1)S(1)}, u32[]{:S(2)}, u32[]{:S(2)}) %collective-permute-start.9) | collective-permute-done | bytes 196640 | tf_op jit(solution)/shard_map/ppermute | solution.py:316
  40.8 0.0 copy-done.6
  40.8 0.0 copy-done.1
  40.8 0.0 copy-done.9
  40.8 7.7 %near.1.refs_4_ = f32[512,512]{1,0:T(8,128)S(1)} custom-call(s32[4,4,9]{2,1,0:T(4,128)S(1)} %copy-done.9, bf16[4,4,32,512]{3,2,1,0:T(8,128)(2,1)S(1)} %copy-done.1, bf16[1,6,32,512]{3,2,1,0:T(8,128)(2,1)S(1)} %collective-permute-done.8.north_hbm, bf16[1,6,32,512]{3,2,1,0:T(8,128)(2,1)S(1)} %collective-permute-done.9.south_hbm, ...), custom_call_target="tpu_custom_call" | custom-call | flops 4831838208 | bytes 8388608 | tf_op jit(solution)/shard_map/near/pallas_call | solution.py:296
  48.5 0.0 copy-done.3
  48.5 0.0 copy-done.5
  48.5 2.0 %spread.2.refs_4_ = f32[512,512]{1,0:T(8,128)S(1)} custom-call(s32[4,2,4]{2,1,0:T(2,128)S(1)} %bitcast.10, s32[2,2048]{1,0:T(2,128)S(1)} %bitcast.7, bf16[2,2048,256]{2,1,0:T(8,128)(2,1)S(1)} %get-tuple-element.8.refs_2_, bf16[8,2,32,128]{3,2,1,0:T(8,128)(2,1)S(1)} %add_convert_fusion.refs_3_, f32[512,512]{1,0:T(8,128)S(1)} %near.1.refs_4_), custom_call_target="tpu_custom_call" | custom-call | flops 1073741824 | bytes 5242880 | tf_op jit(solution)/shard_map/spread/pallas_call | solution.py:221
  50.5 0.0 collective-permute-done.5.refs_3_
  50.5 3.0 %spread.3 = f32[512,512]{1,0:T(8,128)} custom-call(s32[4,2,4]{2,1,0:T(2,128)S(1)} %bitcast.11, s32[2,2048]{1,0:T(2,128)S(1)} %bitcast.8, bf16[2,2048,256]{2,1,0:T(8,128)(2,1)S(1)} %get-tuple-element.8.refs_2_, bf16[8,2,32,128]{3,2,1,0:T(8,128)(2,1)S(1)} %collective-permute-done.5.refs_3_, f32[512,512]{1,0:T(8,128)S(1)} %spread.2.refs_4_), custom_call_target="tpu_custom_call" | custom-call | flops 1073741824 | bytes 5242880 | tf_op jit(solution)/shard_map/spread/pallas_call | solution.py:221
  (8 shorter events, 0.2 us)
Async XLA Ops:
  0.0 1.0 %copy-start = (bf16[4,4,32,512]{3,2,1,0:T(8,128)(2,1)S(1)}, bf16[4,4,32,512]{3,2,1,0:T(8,128)(2,1)}, u32[]{:S(2)}) copy-start(bf16[4,4,32,512]{3,2,1,0:T(8,128)(2,1)} %x_hbm.1) | copy-start | bytes 1572868
  1.0 0.7 %copy-start.2 = (s32[2048,2]{0,1:T(2,128)S(1)}, s32[2048,2]{0,1:T(2,128)}, u32[]{:S(2)}) copy-start(s32[2048,2]{0,1:T(2,128)} %param.11) | copy-start | bytes 49156
  1.8 0.7 %copy-start.4 = (s32[4,4,2]{1,2,0:T(2,128)S(1)}, s32[4,4,2]{1,2,0:T(2,128)}, u32[]{:S(2)}) copy-start(s32[4,4,2]{1,2,0:T(2,128)} %param.10) | copy-start | bytes 388
  2.4 1.6 %copy-start.7 = (bf16[2048,2,256]{2,1,0:T(2,128)(2,1)S(1)}, bf16[2048,2,256]{2,1,0:T(2,128)(2,1)}, u32[]{:S(2)}) copy-start(bf16[2048,2,256]{2,1,0:T(2,128)(2,1)} %refs_4_.1) | copy-start | bytes 6291460
  4.0 0.7 %copy-start.8 = (f32[2048]{0:T(1024)S(1)}, f32[2048]{0:T(1024)}, u32[]{:S(2)}) copy-start(f32[2048]{0:T(1024)} %param.13) | copy-start | bytes 24580
  11.5 5.0 %collective-permute-start = (f32[8,2,32,128]{3,2,1,0:T(8,128)S(1)}, f32[8,2,32,128]{3,2,1,0:T(8,128)S(1)}, u32[]{:S(2)}, u32[]{:S(2)}) collective-permute-start(f32[8,2,32,128]{3,2,1,0:T(8,128)S(1)} %get-tuple-element.10), channel_id=1, source_target_pairs={{0,4},{1,5},{2,6},{3,7},{4,0},{5,1},{6,2},{7,3},{8,12},{9,13},{10,... | collective-permute-start | bytes 786440 | tf_op jit(solution)/shard_map/ppermute | solution.py:334
  11.7 10.5 %collective-permute-start.6 = (bf16[4,1,32,512]{3,2,1,0:T(8,128)(2,1)S(1)}, bf16[4,1,32,512]{3,2,1,0:T(8,128)(2,1)S(1)}, u32[]{:S(2)}, u32[]{:S(2)}) collective-permute-start(bf16[4,1,32,512]{3,2,1,0:T(8,128)(2,1)S(1)} %get-tuple-element.15), channel_id=1, source_target_pairs={{0,1},{1,2},{2,3},{3,0},{4,5},{5,6},{6,7},{7,4},{8,9},{9,10},{10,1... | collective-permute-start | bytes 393224 | tf_op jit(solution)/shard_map/ppermute | solution.py:316
  14.5 10.4 %collective-permute-start.7 = (bf16[4,1,32,512]{3,2,1,0:T(8,128)(2,1)S(1)}, bf16[4,1,32,512]{3,2,1,0:T(8,128)(2,1)S(1)}, u32[]{:S(2)}, u32[]{:S(2)}) collective-permute-start(bf16[4,1,32,512]{3,2,1,0:T(8,128)(2,1)S(1)} %get-tuple-element.16), channel_id=1, source_target_pairs={{0,3},{1,0},{2,1},{3,2},{4,7},{5,4},{6,5},{7,6},{8,11},{9,8},{10,9... | collective-permute-start | bytes 393224 | tf_op jit(solution)/shard_map/ppermute | solution.py:316
  16.5 24.2 %copy-start.6 = (bf16[9,2,2,256,256]{4,3,2,1,0:T(8,128)(2,1)S(1)}, bf16[9,2,2,256,256]{4,3,2,1,0:T(8,128)(2,1)}, u32[]{:S(2)}) copy-start(bf16[9,2,2,256,256]{4,3,2,1,0:T(8,128)(2,1)} %kernel_hbm.1) | copy-start | bytes 14155780
  16.6 4.2 %collective-permute-start.1 = (f16[8,2,32,128]{3,2,1,0:T(8,128)(2,1)S(1)}, f16[8,2,32,128]{3,2,1,0:T(8,128)(2,1)S(1)}, u32[]{:S(2)}, u32[]{:S(2)}) collective-permute-start(f16[8,2,32,128]{3,2,1,0:T(8,128)(2,1)S(1)} %get-tuple-element.11), channel_id=1, source_target_pairs={{0,8},{1,9},{2,10},{3,11},{4,20},{5,21},{6,22},{7,23},{8,0},{9,1},... | collective-permute-start | bytes 393224 | tf_op jit(solution)/shard_map/ppermute | solution.py:334
  17.9 22.9 %copy-start.1 = (bf16[4,4,32,512]{3,2,1,0:T(8,128)(2,1)S(1)}, bf16[4,4,32,512]{3,2,1,0:T(8,128)(2,1)}, u32[]{:S(2)}) copy-start(bf16[4,4,32,512]{3,2,1,0:T(8,128)(2,1)} %x_hbm.1) | copy-start | bytes 1572868
  17.9 22.8 %copy-start.9 = (s32[4,4,9]{2,1,0:T(4,128)S(1)}, s32[4,4,9]{2,1,0:T(4,128)}, u32[]{:S(2)}) copy-start(s32[4,4,9]{2,1,0:T(4,128)} %contact_hbm.1) | copy-start | bytes 1732
  20.8 3.9 %collective-permute-start.2 = (f16[8,2,32,128]{3,2,1,0:T(8,128)(2,1)S(1)}, f16[8,2,32,128]{3,2,1,0:T(8,128)(2,1)S(1)}, u32[]{:S(2)}, u32[]{:S(2)}) collective-permute-start(f16[8,2,32,128]{3,2,1,0:T(8,128)(2,1)S(1)} %fusion), channel_id=1, source_target_pairs={{0,16},{1,17},{2,18},{3,19},{4,12},{5,13},{6,14},{7,15},{8,24},{9,... | collective-permute-start | bytes 393224 | tf_op jit(solution)/shard_map/ppermute | solution.py:334
  24.8 3.9 %collective-permute-start.3 = (f16[8,2,32,128]{3,2,1,0:T(8,128)(2,1)S(1)}, f16[8,2,32,128]{3,2,1,0:T(8,128)(2,1)S(1)}, u32[]{:S(2)}, u32[]{:S(2)}) collective-permute-start(f16[8,2,32,128]{3,2,1,0:T(8,128)(2,1)S(1)} %fusion.2), channel_id=1, source_target_pairs={{0,1},{1,0},{2,3},{3,2},{4,5},{5,4},{6,7},{7,6},{8,9},{9,8},{10,11... | collective-permute-start | bytes 393224 | tf_op jit(solution)/shard_map/ppermute | solution.py:334
  28.8 5.9 %collective-permute-start.4 = (f16[8,2,32,128]{3,2,1,0:T(8,128)(2,1)S(1)}, f16[8,2,32,128]{3,2,1,0:T(8,128)(2,1)S(1)}, u32[]{:S(2)}, u32[]{:S(2)}) collective-permute-start(f16[8,2,32,128]{3,2,1,0:T(8,128)(2,1)S(1)} %fusion.1), channel_id=1, source_target_pairs={{0,2},{1,3},{2,0},{3,1},{4,6},{5,7},{6,4},{7,5},{8,10},{9,11},{10,... | collective-permute-start | bytes 393224 | tf_op jit(solution)/shard_map/ppermute | solution.py:334
  29.2 9.9 %collective-permute-start.8 = (bf16[1,6,32,512]{3,2,1,0:T(8,128)(2,1)S(1)}, bf16[1,6,32,512]{3,2,1,0:T(8,128)(2,1)S(1)}, u32[]{:S(2)}, u32[]{:S(2)}) collective-permute-start(bf16[1,6,32,512]{3,2,1,0:T(8,128)(2,1)S(1)} %pad_maximum_fusion), channel_id=1, source_target_pairs={{0,4},{4,8},{8,12},{12,16},{16,20},{20,24},{24,28},{28,0},{1,5},{5... | collective-permute-start | bytes 589832 | tf_op jit(solution)/shard_map/ppermute | solution.py:316
  34.4 6.3 %collective-permute-start.9 = (bf16[1,6,32,512]{3,2,1,0:T(8,128)(2,1)S(1)}, bf16[1,6,32,512]{3,2,1,0:T(8,128)(2,1)S(1)}, u32[]{:S(2)}, u32[]{:S(2)}) collective-permute-start(bf16[1,6,32,512]{3,2,1,0:T(8,128)(2,1)S(1)} %pad_maximum_fusion.1), channel_id=1, source_target_pairs={{0,28},{4,0},{8,4},{12,8},{16,12},{20,16},{24,20},{28,24},{1,29},{... | collective-permute-start | bytes 589832 | tf_op jit(solution)/shard_map/ppermute | solution.py:316
  34.8 13.7 %copy-start.3 = (s32[2048,2]{0,1:T(2,128)S(1)}, s32[2048,2]{0,1:T(2,128)}, u32[]{:S(2)}) copy-start(s32[2048,2]{0,1:T(2,128)} %param.11) | copy-start | bytes 49156
  34.8 13.7 %copy-start.5 = (s32[4,4,2]{1,2,0:T(2,128)S(1)}, s32[4,4,2]{1,2,0:T(2,128)}, u32[]{:S(2)}) copy-start(s32[4,4,2]{1,2,0:T(2,128)} %param.10) | copy-start | bytes 388
  34.8 15.7 %collective-permute-start.5 = (bf16[8,2,32,128]{3,2,1,0:T(8,128)(2,1)S(1)}, bf16[8,2,32,128]{3,2,1,0:T(8,128)(2,1)S(1)}, u32[]{:S(2)}, u32[]{:S(2)}) collective-permute-start(bf16[8,2,32,128]{3,2,1,0:T(8,128)(2,1)S(1)} %add_convert_fusion.refs_3_), channel_id=1, source_target_pairs={{0,4},{1,5},{2,6},{3,7},{4,0},{5,1},{6,2},{7,3},{8,12},{9,13},{10,... | collective-permute-start | bytes 393224 | tf_op jit(solution)/shard_map/ppermute | solution.py:334

commit v2 on v1

v2 whole, which is shorter than its diff:
```python
import math

import jax
import jax.numpy as jnp
from jax import lax
from jax.experimental import pallas as pl
from jax.experimental.pallas import tpu as pltpu
from jax.sharding import PartitionSpec as P

Q = 16
LANES = 128
TILE = 256

bloch_row = 0.3
bloch_col = 0.17

F32 = jnp.float32
BF16 = jnp.bfloat16
NT = (((1,), (1,)), ((), ()))
HBM = pl.BlockSpec(memory_space=pltpu.MemorySpace.HBM)
VMEM = pl.BlockSpec(memory_space=pltpu.MemorySpace.VMEM)
SMEM = pl.BlockSpec(memory_space=pltpu.MemorySpace.SMEM)


def params(mib):
    return pltpu.CompilerParams(vmem_limit_bytes=mib << 20)


def cost(flops, size):
    return pl.CostEstimate(flops=flops, bytes_accessed=size, transcendentals=0)


def unit(turn):
    y = math.pi * turn
    z = y * y
    even = [(-1) ** k / math.factorial(2 * k) for k in range(8)]
    odd = [(-1) ** k / math.factorial(2 * k + 1) for k in range(8)]
    c = even[7]
    s = odd[7]
    for k in range(6, -1, -1):
        c = c * z + even[k]
        s = s * z + odd[k]
    s = s * y
    return 1.0 - 2.0 * (s * s), 2.0 * (s * c)


def fine(shift, lanes):
    rows, cols = shift.shape[0], shift.shape[2]
    first_row = lax.axis_index("row") * rows
    first_col = lax.axis_index("col") * cols
    spot = lax.broadcasted_iota(jnp.int32, (rows * cols, lanes), 0)
    fr = jnp.zeros(spot.shape, jnp.int32)
    fc = fr
    for p in range(rows * cols):
        r, c = p // cols, p % cols
        fr = jnp.where(spot == p, Q * (first_row + r) + shift[r, 0, c], fr)
        fc = jnp.where(spot == p, Q * (first_col + c) + shift[r, 1, c], fc)
    return fr, fc


def phases(fr, fc, index, row_mod, col_mod):
    turn_row = ((index[0:1] * fr) & (row_mod - 1)).astype(F32) * (1.0 / row_mod)
    turn_col = ((index[1:2] * fc) & (col_mod - 1)).astype(F32) * (1.0 / col_mod)
    drift = (bloch_row / row_mod) * fr.astype(F32) + (bloch_col / col_mod) * fc.astype(F32)
    turn = turn_row + turn_col + drift
    return unit(turn - jnp.round(turn))


def real_form(form, first, tile):
    re = form[0, first : first + tile, :]
    im = form[1, first : first + tile, :]
    upper = jnp.concatenate([re, -im], axis=1)
    lower = jnp.concatenate([im, re], axis=1)
    return jnp.concatenate([upper, lower], axis=0)


def project_body(x_hbm, shift_hbm, index_hbm, weight_hbm, contact_hbm, wave_hbm, kernel_hbm,
                 mine_ref, other_ref, mine_hbm, other_hbm, trig_ref, xs, mask_ref, middle_ref, sides_ref,
                 form_mine, form_other, form_sem, both, contact, shift, index_ref, weight_ref, g, sem, gsem,
                 *, tile, row_mod, col_mod, scale):
    waves = wave_hbm.shape[0]
    half = waves // 2
    width = wave_hbm.shape[2]
    n = shift.shape[0] * shift.shape[2]
    sources = x_hbm.shape[0] // n
    core = lax.axis_index("row") & 1
    small = [
        pltpu.make_async_copy(src, dst, sem.at[k])
        for k, (src, dst) in enumerate(
            (
                (shift_hbm, shift), (index_hbm, index_ref), (weight_hbm, weight_ref), (x_hbm, xs),
                (contact_hbm, contact), (kernel_hbm.at[4], middle_ref.at[0]),
                (kernel_hbm.at[3], sides_ref.at[0]), (kernel_hbm.at[5], sides_ref.at[1]),
            )
        )
    ]
    for c in small[:4]:
        c.start()
    steps = []
    for t in range(waves // tile):
        flip = 1 if t < waves // tile // 2 else 0
        inside = (t * tile) % half
        first = pl.multiple_of((core ^ flip) * half + inside, tile)
        pair = [pltpu.make_async_copy(wave_hbm.at[pl.ds(first, tile)], g.at[t], gsem.at[t])]
        for c in pair:
            c.start()
        steps.append((flip, inside, first, pair))
    for c in small[4:]:
        c.start()
    a = lax.broadcasted_iota(jnp.int32, (2 * LANES, 2 * LANES), 0)
    b = lax.broadcasted_iota(jnp.int32, (2 * LANES, 2 * LANES), 1)
    sort = jnp.where(b == jnp.where(a < LANES, 2 * a, 2 * (a - LANES) + 1), 1.0, 0.0).astype(BF16)
    for c in small[:3]:
        c.wait()
    fr, fc = fine(shift, tile)
    def unmix(t):
        flip, inside, first, pair = steps[t]
        if t == 0:
            pair[0].wait()
        if t == 1:
            for step in steps[1:]:
                step[3][0].wait()
        form = form_other if flip else form_mine
        for k in range(tile // LANES):
            mixed = g[t, k * LANES : (k + 1) * LANES].reshape(2 * LANES, width)
            d = jnp.dot(sort, mixed, preferred_element_type=F32).astype(BF16)
            at = slice(inside + k * LANES, inside + (k + 1) * LANES)
            form[0, at, :] = d[:LANES]
            form[1, at, :] = d[LANES:]

        copies = [
            pltpu.make_async_copy(
                form.at[k, pl.ds(inside, tile)],
                (other_hbm if flip else mine_hbm).at[k, pl.ds(inside, tile)],
                form_sem.at[t, k],
            )
            for k in range(2)
        ]
        for c in copies:
            c.start()
        return copies

    def multiply(t):
        flip, inside, first, pair = steps[t]
        form = form_other if flip else form_mine
        both[t % 2] = lax.dot_general(xs[...], real_form(form, inside, tile), NT, preferred_element_type=F32)

    def angles(t):
        flip, inside, first, pair = steps[t]
        at = pl.ds(first, tile)
        cos, sin = phases(fr, fc, index_ref[:, at], row_mod, col_mod)
        trig_ref[0, :, at] = cos
        trig_ref[1, :, at] = sin

    def add(t):
        flip, inside, first, pair = steps[t]
        at = pl.ds(first, tile)
        ar = jnp.zeros((sources, tile), F32)
        ai = ar
        for p in range(n):
            here = slice(p * sources, (p + 1) * sources)
            u, v = both[t % 2, here, :tile], both[t % 2, here, tile:]
            cp, sp = trig_ref[0, p : p + 1, at], trig_ref[1, p : p + 1, at]
            ar = ar + (cp * u - sp * v)
            ai = ai + (cp * v + sp * u)
        s = scale * weight_ref[:, at]
        ar = ar * s
        ai = ai * s
        out = other_ref if flip else mine_ref
        for k in range(tile // LANES):
            out[inside // LANES + k, 0] = ar[:, LANES * k : LANES * (k + 1)]
            out[inside // LANES + k, 1] = ai[:, LANES * k : LANES * (k + 1)]

    count = len(steps)
    angles(0)
    stores = unmix(0)
    small[3].wait()
    for t in range(count):
        if t + 1 < count:
            stores += unmix(t + 1)
        multiply(t)
        if t + 1 < count:
            angles(t + 1)
        if t > 0:
            add(t - 1)
    add(count - 1)
    for c in small[4:] + stores:
        c.wait()
    cols = shift.shape[2]
    for o in range(mask_ref.shape[0]):
        for p in range(n):
            chosen = jnp.full((1, LANES), contact[p // cols, p % cols, o], jnp.int32)
            mask_ref[o, p : p + 1, :] = chosen.astype(F32)


def in_hbm(*arrays):
    return [pltpu.with_memory_space_constraint(a, pltpu.MemorySpace.HBM) for a in arrays]


def project(x, shift, index, weight, contact, wave_form, near_kernel, row_mod, col_mod, scale, tile=TILE):
    waves, _, width = wave_form.shape
    n = shift.shape[0] * shift.shape[2]
    sources = x.shape[0] // n
    half = pltpu.VMEM((waves // 2 // LANES, 2, sources, LANES), F32)

    form = pltpu.HBM((2, waves // 2, width), BF16)

    def body(*refs):
        project_body(*refs, tile=tile, row_mod=row_mod, col_mod=col_mod, scale=scale)

    return pl.pallas_call(
        body,
        in_specs=[HBM] * 7,
        out_specs=[VMEM] * 2 + [HBM] * 2 + [VMEM] * 5,
        out_shape=[
            half,
            half,
            form,
            form,
            pltpu.VMEM((2, n, waves), F32),
            pltpu.VMEM(x.shape, BF16),
            pltpu.VMEM((contact.shape[2], n, LANES), F32),
            pltpu.VMEM((1,) + near_kernel.shape[1:], BF16),
            pltpu.VMEM((2,) + near_kernel.shape[1:], BF16),
        ],
        scratch_shapes=[
            pltpu.VMEM((2, waves // 2, width), BF16),
            pltpu.VMEM((2, waves // 2, width), BF16),
            pltpu.SemaphoreType.DMA((waves // tile, 2)),
            pltpu.VMEM((2, x.shape[0], 2 * tile), F32),
            pltpu.SMEM(contact.shape, jnp.int32),
            pltpu.SMEM(shift.shape, jnp.int32),
            pltpu.VMEM(index.shape, jnp.int32),
            pltpu.VMEM(weight.shape, F32),
            pltpu.VMEM((waves // tile, tile, 2, width), BF16),
            pltpu.SemaphoreType.DMA((8,)),
            pltpu.SemaphoreType.DMA((waves // tile,)),
        ],
        compiler_params=params(24),
        cost_estimate=cost(8 * x.shape[0] * width * waves, 5 << 20),
        name="project",
    )(*in_hbm(x, shift, index, weight, contact, wave_form, near_kernel))


def spread_body(trig_ref, form_ref, coeff_ref, base_ref, out_ref, lhs, *, flip, tile):
    waves = trig_ref.shape[2]
    half = waves // 2
    n = trig_ref.shape[1]
    sources = coeff_ref.shape[2]
    core = (lax.axis_index("row") & 1) ^ flip
    for t in range(half // tile):
        at = pl.ds(pl.multiple_of(core * half + t * tile, tile), tile)
        cos, sin = trig_ref[0, :, at], trig_ref[1, :, at]
        groups = range(t * tile // LANES, (t + 1) * tile // LANES)
        wr = jnp.concatenate([coeff_ref[k, 0].astype(F32) for k in groups], axis=1)
        wi = jnp.concatenate([coeff_ref[k, 1].astype(F32) for k in groups], axis=1)
        for p in range(n):
            cp, sp = cos[p : p + 1], sin[p : p + 1]
            here = slice(p * sources, (p + 1) * sources)
            lhs[t, here, :tile] = (cp * wr + sp * wi).astype(BF16)
            lhs[t, here, tile:] = (cp * wi - sp * wr).astype(BF16)
        src = base_ref if t == 0 else out_ref
        w = real_form(form_ref, t * tile, tile)
        out_ref[...] = src[...] + jnp.dot(lhs[t], w, preferred_element_type=F32)


def spread(trig, form, coeff, base, flip, tile=TILE):
    half = trig.shape[2] // 2

    def body(*refs):
        spread_body(*refs, flip=flip, tile=tile)

    return pl.pallas_call(
        body,
        in_specs=[VMEM] * 4,
        out_specs=VMEM,
        out_shape=jax.ShapeDtypeStruct(base.shape, F32),
        scratch_shapes=[pltpu.VMEM((half // tile, base.shape[0], 2 * tile), BF16)],
        compiler_params=params(24),
        cost_estimate=cost(4 * base.shape[0] * base.shape[1] * half, 5 << 20),
        name="spread",
    )(trig, form, coeff, base)


def near_body(*refs, offsets, coming, halo, after):
    mask_ref, x = refs[:2]
    halos = refs[2 : 2 + halo]
    held, refs = refs[2 + halo], refs[3 + halo :]
    if coming:
        kernel_hbm, refs = refs[0], refs[1:]
    if after:
        base_ref, refs = refs[0], refs[1:]
    out_ref, refs = refs[0], refs[1:]
    copies = []
    if coming:
        copies = [
            pltpu.make_async_copy(kernel_hbm.at[o], refs[0].at[k], refs[2].at[k]) for k, o in enumerate(coming)
        ]
        for c in copies:
            c.start()
        refs = refs[1:]
    lhs = refs[0]
    rows, cols, sources, full = x.shape
    classes = held.shape[1]

    def block(r, c):
        if r < 0:
            return halos[2][0, c + 1]
        if r >= rows:
            return halos[3][0, c + 1]
        if c < 0:
            return halos[0][r, 0]
        if c >= cols:
            return halos[1][r, 0]
        return x[r, c]

    def gather(k):
        o = offsets[k]
        for p in range(rows * cols):
            r, c = p // cols, p % cols
            here = slice(p * sources, (p + 1) * sources)
            xb = block(r + o // 3 - 1, c + o % 3 - 1)
            m = jnp.broadcast_to(mask_ref[o, p : p + 1, :], (sources, LANES)).astype(BF16)
            second = xb * jnp.concatenate([m] * (full // LANES), axis=1)
            lhs[k % 2, here, :full] = xb - second
            lhs[k % 2, here, full:] = second

    for k, o in enumerate(offsets):
        gather(k)
        upper, lower = [], []
        for v in range(classes):
            re, im = held[k, v, 0], held[k, v, 1]
            upper += [re, -im]
            lower += [im, re]
        w = jnp.concatenate([jnp.concatenate(upper, axis=1), jnp.concatenate(lower, axis=1)], axis=0)
        product = lax.dot_general(lhs[k % 2], w, NT, preferred_element_type=F32)
        if k == 0 and not after:
            out_ref[...] = product
        else:
            out_ref[...] = (base_ref if k == 0 else out_ref)[...] + product


    for c in copies:
        c.wait()


def near_field(offsets, coming, mask, x, halos, held, kernel, base=None):
    rows, cols, sources, full = x.shape
    m = rows * cols * sources
    classes = kernel.shape[1]
    after = base is not None

    def body(*refs):
        near_body(*refs, offsets=offsets, coming=coming, halo=len(halos), after=after)

    operands = [mask, x, *halos, held]
    specs = [VMEM] * len(operands)
    out = [pltpu.VMEM((m, full), F32)]
    scratch = [pltpu.VMEM((2, m, classes * full), BF16)]
    if coming:
        operands += in_hbm(kernel)
        specs += [HBM]
        out += [pltpu.VMEM((len(coming),) + kernel.shape[1:], BF16)]
        scratch += [pltpu.SemaphoreType.DMA((len(coming),))]
    return pl.pallas_call(
        body,
        in_specs=specs + [VMEM] * after,
        out_specs=[VMEM] * len(out),
        out_shape=out,
        scratch_shapes=scratch,
        compiler_params=params(24),
        cost_estimate=cost(2 * len(offsets) * classes * m * full * full, 4 << 20),
        name="near",
    )(*operands, *[base] * after)


def paired(low, high, axis):
    count = lax.axis_size(axis)
    odd = (lax.axis_index(axis) & 1) == 1
    inner = [(i, i ^ 1) for i in range(count)]
    outer = [(i, (i + 1 if i & 1 else i - 1) % count) for i in range(count)]

    def first():
        return lax.ppermute(jnp.where(odd, low, high), axis, inner)

    def second():
        return lax.ppermute(jnp.where(odd, high, low), axis, outer)

    def sort(a, b):
        return jnp.where(odd, a, b), jnp.where(odd, b, a)

    return first, second, sort


def bits(count, first):
    out = []
    while first < count:
        out.append(first)
        first *= 2
    return out


def exchange(value, dims):
    n_row, n_col = lax.axis_size("row"), lax.axis_size("col")
    pairs = []
    for r in range(n_row):
        for c in range(n_col):
            dr, dc = dims[r & 1]
            pairs.append((r * n_col + c, (r ^ dr) * n_col + (c ^ dc)))
    return lax.ppermute(value, ("row", "col"), pairs)


def pack(value):
    return (value * (128.0 * lax.rsqrt(jnp.maximum(jnp.abs(value), 1e-36)))).astype(jnp.float16)


def unpack(got):
    root = got.astype(F32)
    return root * jnp.abs(root) * (1.0 / 128.0**2)


def local(field, near_kernel, contact, pillar_shift, wave_index, wave_form, wave_weight):
    rows, cols, sources, full = field.shape
    waves = wave_form.shape[0]
    n_row, n_col = lax.axis_size("row"), lax.axis_size("col")
    row_mod = Q * rows * n_row
    col_mod = Q * cols * n_col
    scale = math.sqrt(full // 2 / (waves * rows * n_row * cols * n_col))
    shift = jnp.swapaxes(pillar_shift, 1, 2)
    index = wave_index.T
    weight = wave_weight.reshape(1, -1)
    mine, other, form, form_other, trig, cells, mask, middle, sides = project(
        field.reshape(-1, full), shift, index, weight, contact, wave_form, near_kernel, row_mod, col_mod, scale
    )
    cells = cells.reshape(field.shape)
    total = mine + exchange(other, ((1, 0), (1, 0)))
    by_row = [(b, 0) for b in bits(n_row, 2)]
    by_col = [(0, b) for b in bits(n_col, 1)]
    steps = list(zip(by_row + by_col, by_row[::-1] + by_col[::-1]))
    tie = lax.optimization_barrier

    payload, here = tie((pack(total), cells))
    got = exchange(payload, steps[0])
    _, second, _ = paired(here[:, :1], here[:, cols - 1 :], "col")
    outer = second()
    total = total + unpack(got)

    payload, here = tie((pack(total), here))
    got = exchange(payload, steps[1])
    first, _, sort = paired(here[:, :1], here[:, cols - 1 :], "col")
    inner = first()
    out, upper = near_field((4,), (0, 1, 2), mask, here, (), middle, near_kernel)
    total = total + unpack(got)

    west, east = sort(inner, outer)
    payload, out = tie((pack(total), out))
    got = exchange(payload, steps[2])
    low = jnp.concatenate([west[:1], cells[:1], east[:1]], axis=1)
    high = jnp.concatenate([west[-1:], cells[-1:], east[-1:]], axis=1)
    first, second, sort = paired(low, high, "row")
    north, south = sort(first(), second())
    out, lower = near_field((3, 5), (6, 7, 8), mask, cells, (west, east), sides, near_kernel, out)
    total = total + unpack(got)

    payload, out = tie((pack(total), out))
    got = exchange(payload, steps[3])
    halos = (west, east, north, south)
    (out,) = near_field((0, 1, 2), (), mask, cells, halos, upper, near_kernel, out)
    (out,) = near_field((6, 7, 8), (), mask, cells, halos, lower, near_kernel, out)
    total = total + unpack(got)
    for dims in steps[4:]:
        total = total + unpack(exchange(pack(total), dims))
    weighted, out = tie((total.astype(BF16), out))
    weighted_other = exchange(weighted, ((1, 0), (1, 0)))
    out = spread(trig, form, weighted, out, 0)
    out = spread(trig, form_other, weighted_other, out, 1)
    return out.reshape(field.shape)


def solution(mesh):
    placed = (
        P("row", "col", None, None),
        P(),
        P("row", "col", None),
        P("row", "col", None),
        P(),
        P(),
        P(),
    )
    return jax.shard_map(
        local, mesh=mesh, in_specs=placed, out_specs=P("row", "col", None, None), check_vma=False
    )
```

time: 54 us -> 37 us (0.69)
  the two profiles are of different devices: /device:TPU:1 before, /device:TPU:0 now
where the time goes in v2:
time: 37 us; the launch traced here: 36.8 us
  Pallas kernels  16.9 us (46%)
  starting transfers between devices  16.2 us (44%)
  waiting for transfers between devices  2.65 us (7%)
  other arithmetic  0.88 us (2%)
    ppermute x6, starting transfers between devices, exchange(): return lax.ppermute(value, ('row', 'col'), pairs)  9.42 us
    pallas_call x4, Pallas kernels, near_field(): pl.pallas_call(body, in_specs=specs + [VMEM] * after, out_specs=[VMEM] *...  7.52 us
    pallas_call x1, Pallas kernels, project(): pl.pallas_call(body, in_specs=[HBM] * 7, out_specs=[VMEM] * 2 + [HBM] * 2...  5.88 us
    ppermute x2, starting transfers between devices, second(): return lax.ppermute(jnp.where(odd, high, low), axis, outer)  4.94 us
    pallas_call x2, Pallas kernels, spread(): pl.pallas_call(body, in_specs=[VMEM] * 4, out_specs=VMEM, out_shape=jax.S...  3.49 us
    ppermute x2, starting transfers between devices, first(): return lax.ppermute(jnp.where(odd, low, high), axis, inner)  1.82 us
    ppermute x6, waiting for transfers between devices, exchange(): return lax.ppermute(value, ('row', 'col'), pairs)  1.65 us
    ppermute x2, waiting for transfers between devices, second(): return lax.ppermute(jnp.where(odd, high, low), axis, outer)  0.98 us
  transfers between devices with their start and end apart: 10, of which 5 were waited for; matrix products, arithmetic and copies ran while one was open for 2% of the time, Pallas kernels for 24%

profile of v2, /device:TPU:0, one launch (start us, length us, event | category | flops | bytes accessed | tf_op | source)
XLA Modules:
  0.0 36.8 jit_solution(6508754250113758755)
XLA Ops:
  0.0 5.9 %project.1 = (f32[8,2,32,128]{3,2,1,0:T(8,128)S(1)}, f32[8,2,32,128]{3,2,1,0:T(8,128)S(1)}, bf16[2,1024,256]{2,1,0:T(8,128)(2,1)}, bf16[2,1024,256]{2,1,0:T(8,12...) custom-call(bf16[512,512]{1,0:T(8,128)(2,1)} %bitcast.16, ...), custom_call_target="tpu_custom_call" | custom-call | flops 2147483648 | bytes 5242880 | tf_op jit(solution)/shard_map/project/pallas_call | solution.py:211
  5.9 0.5 %collective-permute-start = (f32[8,2,32,128]{3,2,1,0:T(8,128)S(1)}, f32[8,2,32,128]{3,2,1,0:T(8,128)S(1)}, u32[]{:S(2)}, u32[]{:S(2)}) collective-permute-start(f32[8,2,32,128]{3,2,1,0:T(8,128)S(1)} %get-tuple-element.31), channel_id=1, source_target_pairs={{0,4},{1,5},{2,6},{3,7},{4,0},{5,1},{6,2},{7,3},{8,12},{9,13},{10,... | collective-permute-start | bytes 786440 | tf_op jit(solution)/shard_map/ppermute | solution.py:410
  6.4 1.1 %collective-permute-done = f32[8,2,32,128]{3,2,1,0:T(8,128)S(1)} collective-permute-done((f32[8,2,32,128]{3,2,1,0:T(8,128)S(1)}, f32[8,2,32,128]{3,2,1,0:T(8,128)S(1)}, u32[]{:S(2)}, u32[]{:S(2)}) %collective-permute-start) | collective-permute-done | bytes 262176 | tf_op jit(solution)/shard_map/ppermute | solution.py:410
  7.6 0.1 multiply_convert_fusion.3
  7.7 2.9 %collective-permute-start.1 = (f16[8,2,32,128]{3,2,1,0:T(8,128)(2,1)S(1)}, f16[8,2,32,128]{3,2,1,0:T(8,128)(2,1)S(1)}, u32[]{:S(2)}, u32[]{:S(2)}) collective-permute-start(f16[8,2,32,128]{3,2,1,0:T(8,128)(2,1)S(1)} %get-tuple-element.33), channel_id=1, source_target_pairs={{0,8},{1,9},{2,10},{3,11},{4,20},{5,21},{6,22},{7,23},{8,0},{9,1},... | collective-permute-start | bytes 393224 | tf_op jit(solution)/shard_map/ppermute | solution.py:410
  10.6 3.7 %collective-permute-start.5 = (bf16[4,1,32,512]{3,2,1,0:T(8,128)(2,1)S(1)}, bf16[4,1,32,512]{3,2,1,0:T(8,128)(2,1)S(1)}, u32[]{:S(2)}, u32[]{:S(2)}) collective-permute-start(bf16[4,1,32,512]{3,2,1,0:T(8,128)(2,1)S(1)} %slice_select_fusion), channel_id=1, source_target_pairs={{0,3},{1,2},{2,1},{3,0},{4,7},{5,6},{6,5},{7,4},{8,11},{9,10},{10,... | collective-permute-start | bytes 393224 | tf_op jit(solution)/shard_map/ppermute | solution.py:387
  14.3 0.0 collective-permute-done.1
  14.3 0.1 multiply_convert_fusion.2
  14.4 1.6 %collective-permute-start.2 = (f16[8,2,32,128]{3,2,1,0:T(8,128)(2,1)S(1)}, f16[8,2,32,128]{3,2,1,0:T(8,128)(2,1)S(1)}, u32[]{:S(2)}, u32[]{:S(2)}) collective-permute-start(f16[8,2,32,128]{3,2,1,0:T(8,128)(2,1)S(1)} %multiply_convert_fusion.2), channel_id=1, source_target_pairs={{0,16},{1,17},{2,18},{3,19},{4,12},{5,13},{6,14},{7,15},{8,24},{9,... | collective-permute-start | bytes 393224 | tf_op jit(solution)/shard_map/ppermute | solution.py:410
  16.0 1.4 %collective-permute-start.4 = (bf16[4,1,32,512]{3,2,1,0:T(8,128)(2,1)S(1)}, bf16[4,1,32,512]{3,2,1,0:T(8,128)(2,1)S(1)}, u32[]{:S(2)}, u32[]{:S(2)}) collective-permute-start(bf16[4,1,32,512]{3,2,1,0:T(8,128)(2,1)S(1)} %slice_select_fusion.1), channel_id=1, source_target_pairs={{0,1},{1,0},{2,3},{3,2},{4,5},{5,4},{6,7},{7,6},{8,9},{9,8},{10,11... | collective-permute-start | bytes 393224 | tf_op jit(solution)/shard_map/ppermute | solution.py:384
  17.4 1.6 %near.4 = (f32[512,512]{1,0:T(8,128)S(1)}, bf16[3,2,2,256,256]{4,3,2,1,0:T(8,128)(2,1)S(1)}) custom-call(f32[9,16,128]{2,1,0:T(8,128)S(1)} %get-tuple-element.36.refs_0_, bf16[4,4,32,512]{3,2,1,0:T(8,128)(2,1)S(1)} %bitcast.10, bf16[1,2,2,256,256]{4,3,2,1,0:T(8,128)(2,1)S(1)} %get-tuple-element.38.refs_2_, bf16[9,2,2,256,256]{4,3,2,1,0:T(8,128)(2,1)} %refs_5_.3), custom_call_target="tpu_custom_call" | custom-call | flops 536870912 | bytes 4194304 | tf_op jit(solution)/shard_map/near/pallas_call | solution.py:365
  19.0 0.4 %collective-permute-done.2 = f16[8,2,32,128]{3,2,1,0:T(8,128)(2,1)S(1)} collective-permute-done((f16[8,2,32,128]{3,2,1,0:T(8,128)(2,1)S(1)}, f16[8,2,32,128]{3,2,1,0:T(8,128)(2,1)S(1)}, u32[]{:S(2)}, u32[]{:S(2)}) %collective-permute-start.2) | collective-permute-done | bytes 131104 | tf_op jit(solution)/shard_map/ppermute | solution.py:410
  19.4 0.2 multiply_convert_fusion.1
  19.6 1.4 %collective-permute-start.3 = (f16[8,2,32,128]{3,2,1,0:T(8,128)(2,1)S(1)}, f16[8,2,32,128]{3,2,1,0:T(8,128)(2,1)S(1)}, u32[]{:S(2)}, u32[]{:S(2)}) collective-permute-start(f16[8,2,32,128]{3,2,1,0:T(8,128)(2,1)S(1)} %multiply_convert_fusion.1), channel_id=1, source_target_pairs={{0,1},{1,0},{2,3},{3,2},{4,6},{5,7},{6,4},{7,5},{8,9},{9,8},{10,11... | collective-permute-start | bytes 393224 | tf_op jit(solution)/shard_map/ppermute | solution.py:410
  21.0 0.0 collective-permute-done.5
  21.0 0.0 collective-permute-done.4
  21.1 0.1 broadcast_select_fusion.2
  21.1 1.3 %collective-permute-start.8 = (bf16[1,6,32,512]{3,2,1,0:T(8,128)(2,1)S(1)}, bf16[1,6,32,512]{3,2,1,0:T(8,128)(2,1)S(1)}, u32[]{:S(2)}, u32[]{:S(2)}) collective-permute-start(bf16[1,6,32,512]{3,2,1,0:T(8,128)(2,1)S(1)} %get-tuple-element.57), channel_id=1, source_target_pairs={{0,28},{4,8},{8,4},{12,16},{16,12},{20,24},{24,20},{28,0},{1,29},{... | collective-permute-start | bytes 589832 | tf_op jit(solution)/shard_map/ppermute | solution.py:387
  22.4 0.4 %collective-permute-start.7 = (bf16[1,6,32,512]{3,2,1,0:T(8,128)(2,1)S(1)}, bf16[1,6,32,512]{3,2,1,0:T(8,128)(2,1)S(1)}, u32[]{:S(2)}, u32[]{:S(2)}) collective-permute-start(bf16[1,6,32,512]{3,2,1,0:T(8,128)(2,1)S(1)} %get-tuple-element.58), channel_id=1, source_target_pairs={{0,4},{4,0},{8,12},{12,8},{16,20},{20,16},{24,28},{28,24},{1,5},{5... | collective-permute-start | bytes 589832 | tf_op jit(solution)/shard_map/ppermute | solution.py:384
  22.8 2.3 %near.5 = (f32[512,512]{1,0:T(8,128)S(1)}, bf16[3,2,2,256,256]{4,3,2,1,0:T(8,128)(2,1)S(1)}) custom-call(f32[9,16,128]{2,1,0:T(8,128)S(1)} %get-tuple-element.36.refs_0_, bf16[4,4,32,512]{3,2,1,0:T(8,128)(2,1)S(1)} %bitcast.11, bf16[4,1,32,512]{3,2,1,0:T(8,128)(2,1)S(1)} %get-tuple-element.60.refs_2_, bf16[4,1,32,512]{3,2,1,0:T(8,128)(2,1)S(1)} %get-tuple-element.59.refs_3_, ...), custom_call_target="tpu_custom_call" | custom-call | flops 1073741824 | bytes 4194304 | tf_op jit(solution)/shard_map/near/pallas_call | solution.py:365
  25.1 0.1 collective-permute-done.3
  25.1 0.2 multiply_convert_fusion
  25.3 2.9 %collective-permute-start.6 = (f16[8,2,32,128]{3,2,1,0:T(8,128)(2,1)S(1)}, f16[8,2,32,128]{3,2,1,0:T(8,128)(2,1)S(1)}, u32[]{:S(2)}, u32[]{:S(2)}) collective-permute-start(f16[8,2,32,128]{3,2,1,0:T(8,128)(2,1)S(1)} %multiply_convert_fusion), channel_id=1, source_target_pairs={{0,2},{1,3},{2,0},{3,1},{4,5},{5,4},{6,7},{7,6},{8,10},{9,11},{10,... | collective-permute-start | bytes 393224 | tf_op jit(solution)/shard_map/ppermute | solution.py:410
  28.2 1.0 %collective-permute-done.8 = bf16[1,6,32,512]{3,2,1,0:T(8,128)(2,1)S(1)} collective-permute-done((bf16[1,6,32,512]{3,2,1,0:T(8,128)(2,1)S(1)}, bf16[1,6,32,512]{3,2,1,0:T(8,128)(2,1)S(1)}, u32[]{:S(2)}, u32[]{:S(2)}) %collective-permute-start.8) | collective-permute-done | bytes 196640 | tf_op jit(solution)/shard_map/ppermute | solution.py:387
  29.2 0.0 collective-permute-done.7
  29.2 1.8 %near.6.refs_7_ = f32[512,512]{1,0:T(8,128)S(1)} custom-call(f32[9,16,128]{2,1,0:T(8,128)S(1)} %get-tuple-element.36.refs_0_, bf16[4,4,32,512]{3,2,1,0:T(8,128)(2,1)S(1)} %bitcast.12, bf16[4,1,32,512]{3,2,1,0:T(8,128)(2,1)S(1)} %get-tuple-element.60.refs_2_, bf16[4,1,32,512]{3,2,1,0:T(8,128)(2,1)S(1)} %get-tuple-element.59.refs_3_, ...), custom_call_target="tpu_custom_call" | custom-call | flops 1610612736 | bytes 4194304 | tf_op jit(solution)/shard_map/near/pallas_call | solution.py:365
  31.1 0.0 copy-start.1
  31.1 1.8 %near.7.refs_3_ = f32[512,512]{1,0:T(8,128)S(1)} custom-call(f32[9,16,128]{2,1,0:T(8,128)S(1)} %get-tuple-element.36.refs_0_, bf16[4,4,32,512]{3,2,1,0:T(8,128)(2,1)S(1)} %bitcast.13, bf16[4,1,32,512]{3,2,1,0:T(8,128)(2,1)S(1)} %get-tuple-element.60.refs_2_, bf16[4,1,32,512]{3,2,1,0:T(8,128)(2,1)S(1)} %get-tuple-element.59.refs_3_, ...), custom_call_target="tpu_custom_call" | custom-call | flops 1610612736 | bytes 4194304 | tf_op jit(solution)/shard_map/near/pallas_call | solution.py:365
  32.9 0.0 collective-permute-done.6
  32.9 0.2 fusion.8.refs_2_
  33.1 0.0 copy-start
  33.1 0.1 collective-permute-start.9
  33.2 0.0 copy-done.1
  33.2 1.3 %spread.2.refs_3_ = f32[512,512]{1,0:T(8,128)S(1)} custom-call(f32[2,16,2048]{2,1,0:T(8,128)S(1)} %get-tuple-element.28.refs_0_, bf16[2,1024,256]{2,1,0:T(8,128)(2,1)S(1)} %copy-done.1, bf16[8,2,32,128]{3,2,1,0:T(8,128)(2,1)S(1)} %fusion.8.refs_2_, f32[512,512]{1,0:T(8,128)S(1)} %near.7.refs_3_), custom_call_target="tpu_custom_call" | custom-call | flops 1073741824 | bytes 5242880 | tf_op jit(solution)/shard_map/spread/pallas_call | solution.py:273
  34.5 0.1 collective-permute-done.9.refs_2_
  34.5 0.0 copy-done
  34.6 2.2 %spread.3 = f32[512,512]{1,0:T(8,128)} custom-call(f32[2,16,2048]{2,1,0:T(8,128)S(1)} %get-tuple-element.28.refs_0_, bf16[2,1024,256]{2,1,0:T(8,128)(2,1)S(1)} %copy-done, bf16[8,2,32,128]{3,2,1,0:T(8,128)(2,1)S(1)} %collective-permute-done.9.refs_2_, f32[512,512]{1,0:T(8,128)S(1)} %spread.2.refs_3_), custom_call_target="tpu_custom_call" | custom-call | flops 1073741824 | bytes 5242880 | tf_op jit(solution)/shard_map/spread/pallas_call | solution.py:273
  (6 shorter events, 0.1 us)
Async XLA Ops:
  5.9 1.7 %collective-permute-start = (f32[8,2,32,128]{3,2,1,0:T(8,128)S(1)}, f32[8,2,32,128]{3,2,1,0:T(8,128)S(1)}, u32[]{:S(2)}, u32[]{:S(2)}) collective-permute-start(f32[8,2,32,128]{3,2,1,0:T(8,128)S(1)} %get-tuple-element.31), channel_id=1, source_target_pairs={{0,4},{1,5},{2,6},{3,7},{4,0},{5,1},{6,2},{7,3},{8,12},{9,13},{10,... | collective-permute-start | bytes 786440 | tf_op jit(solution)/shard_map/ppermute | solution.py:410
  7.7 6.6 %collective-permute-start.1 = (f16[8,2,32,128]{3,2,1,0:T(8,128)(2,1)S(1)}, f16[8,2,32,128]{3,2,1,0:T(8,128)(2,1)S(1)}, u32[]{:S(2)}, u32[]{:S(2)}) collective-permute-start(f16[8,2,32,128]{3,2,1,0:T(8,128)(2,1)S(1)} %get-tuple-element.33), channel_id=1, source_target_pairs={{0,8},{1,9},{2,10},{3,11},{4,20},{5,21},{6,22},{7,23},{8,0},{9,1},... | collective-permute-start | bytes 393224 | tf_op jit(solution)/shard_map/ppermute | solution.py:410
  10.6 10.4 %collective-permute-start.5 = (bf16[4,1,32,512]{3,2,1,0:T(8,128)(2,1)S(1)}, bf16[4,1,32,512]{3,2,1,0:T(8,128)(2,1)S(1)}, u32[]{:S(2)}, u32[]{:S(2)}) collective-permute-start(bf16[4,1,32,512]{3,2,1,0:T(8,128)(2,1)S(1)} %slice_select_fusion), channel_id=1, source_target_pairs={{0,3},{1,2},{2,1},{3,0},{4,7},{5,6},{6,5},{7,4},{8,11},{9,10},{10,... | collective-permute-start | bytes 393224 | tf_op jit(solution)/shard_map/ppermute | solution.py:387
  14.4 5.0 %collective-permute-start.2 = (f16[8,2,32,128]{3,2,1,0:T(8,128)(2,1)S(1)}, f16[8,2,32,128]{3,2,1,0:T(8,128)(2,1)S(1)}, u32[]{:S(2)}, u32[]{:S(2)}) collective-permute-start(f16[8,2,32,128]{3,2,1,0:T(8,128)(2,1)S(1)} %multiply_convert_fusion.2), channel_id=1, source_target_pairs={{0,16},{1,17},{2,18},{3,19},{4,12},{5,13},{6,14},{7,15},{8,24},{9,... | collective-permute-start | bytes 393224 | tf_op jit(solution)/shard_map/ppermute | solution.py:410
  16.0 5.0 %collective-permute-start.4 = (bf16[4,1,32,512]{3,2,1,0:T(8,128)(2,1)S(1)}, bf16[4,1,32,512]{3,2,1,0:T(8,128)(2,1)S(1)}, u32[]{:S(2)}, u32[]{:S(2)}) collective-permute-start(bf16[4,1,32,512]{3,2,1,0:T(8,128)(2,1)S(1)} %slice_select_fusion.1), channel_id=1, source_target_pairs={{0,1},{1,0},{2,3},{3,2},{4,5},{5,4},{6,7},{7,6},{8,9},{9,8},{10,11... | collective-permute-start | bytes 393224 | tf_op jit(solution)/shard_map/ppermute | solution.py:384
  19.6 5.5 %collective-permute-start.3 = (f16[8,2,32,128]{3,2,1,0:T(8,128)(2,1)S(1)}, f16[8,2,32,128]{3,2,1,0:T(8,128)(2,1)S(1)}, u32[]{:S(2)}, u32[]{:S(2)}) collective-permute-start(f16[8,2,32,128]{3,2,1,0:T(8,128)(2,1)S(1)} %multiply_convert_fusion.1), channel_id=1, source_target_pairs={{0,1},{1,0},{2,3},{3,2},{4,6},{5,7},{6,4},{7,5},{8,9},{9,8},{10,11... | collective-permute-start | bytes 393224 | tf_op jit(solution)/shard_map/ppermute | solution.py:410
  21.1 8.1 %collective-permute-start.8 = (bf16[1,6,32,512]{3,2,1,0:T(8,128)(2,1)S(1)}, bf16[1,6,32,512]{3,2,1,0:T(8,128)(2,1)S(1)}, u32[]{:S(2)}, u32[]{:S(2)}) collective-permute-start(bf16[1,6,32,512]{3,2,1,0:T(8,128)(2,1)S(1)} %get-tuple-element.57), channel_id=1, source_target_pairs={{0,28},{4,8},{8,4},{12,16},{16,12},{20,24},{24,20},{28,0},{1,29},{... | collective-permute-start | bytes 589832 | tf_op jit(solution)/shard_map/ppermute | solution.py:387
  22.4 6.8 %collective-permute-start.7 = (bf16[1,6,32,512]{3,2,1,0:T(8,128)(2,1)S(1)}, bf16[1,6,32,512]{3,2,1,0:T(8,128)(2,1)S(1)}, u32[]{:S(2)}, u32[]{:S(2)}) collective-permute-start(bf16[1,6,32,512]{3,2,1,0:T(8,128)(2,1)S(1)} %get-tuple-element.58), channel_id=1, source_target_pairs={{0,4},{4,0},{8,12},{12,8},{16,20},{20,16},{24,28},{28,24},{1,5},{5... | collective-permute-start | bytes 589832 | tf_op jit(solution)/shard_map/ppermute | solution.py:384
  25.3 7.6 %collective-permute-start.6 = (f16[8,2,32,128]{3,2,1,0:T(8,128)(2,1)S(1)}, f16[8,2,32,128]{3,2,1,0:T(8,128)(2,1)S(1)}, u32[]{:S(2)}, u32[]{:S(2)}) collective-permute-start(f16[8,2,32,128]{3,2,1,0:T(8,128)(2,1)S(1)} %multiply_convert_fusion), channel_id=1, source_target_pairs={{0,2},{1,3},{2,0},{3,1},{4,5},{5,4},{6,7},{7,6},{8,10},{9,11},{10,... | collective-permute-start | bytes 393224 | tf_op jit(solution)/shard_map/ppermute | solution.py:410
  31.1 2.1 %copy-start.1 = (bf16[2,1024,256]{2,1,0:T(8,128)(2,1)S(1)}, bf16[2,1024,256]{2,1,0:T(8,128)(2,1)}, u32[]{:S(2)}) copy-start(bf16[2,1024,256]{2,1,0:T(8,128)(2,1)} %get-tuple-element.49.refs_1_) | copy-start | bytes 3145732
  33.1 1.4 %copy-start = (bf16[2,1024,256]{2,1,0:T(8,128)(2,1)S(1)}, bf16[2,1024,256]{2,1,0:T(8,128)(2,1)}, u32[]{:S(2)}) copy-start(bf16[2,1024,256]{2,1,0:T(8,128)(2,1)} %get-tuple-element.29.refs_1_) | copy-start | bytes 3145732
  33.1 1.4 %collective-permute-start.9 = (bf16[8,2,32,128]{3,2,1,0:T(8,128)(2,1)S(1)}, bf16[8,2,32,128]{3,2,1,0:T(8,128)(2,1)S(1)}, u32[]{:S(2)}, u32[]{:S(2)}) collective-permute-start(bf16[8,2,32,128]{3,2,1,0:T(8,128)(2,1)S(1)} %fusion.8.refs_2_), channel_id=1, source_target_pairs={{0,4},{1,5},{2,6},{3,7},{4,0},{5,1},{6,2},{7,3},{8,12},{9,13},{10,... | collective-permute-start | bytes 393224 | tf_op jit(solution)/shard_map/ppermute | solution.py:410

commit v3 on v2

--- a/solution.py
+++ b/solution.py
@@ -74,9 +74,9 @@
     return jnp.concatenate([upper, lower], axis=0)
 
 
-def project_body(x_hbm, shift_hbm, index_hbm, weight_hbm, contact_hbm, wave_hbm, kernel_hbm,
-                 mine_ref, other_ref, mine_hbm, other_hbm, trig_ref, xs, mask_ref, middle_ref, sides_ref,
-                 form_mine, form_other, form_sem, both, contact, shift, index_ref, weight_ref, g, sem, gsem,
+def project_body(x_hbm, shift_hbm, index_hbm, weight_hbm, contact_hbm, wave_hbm,
+                 mine_ref, other_ref, form_mine, form_other, trig_ref, xs, mask_ref,
+                 both, contact, shift, index_ref, weight_ref, g, sem, gsem,
                  *, tile, row_mod, col_mod, scale):
     waves = wave_hbm.shape[0]
     half = waves // 2
@@ -89,8 +89,7 @@
         for k, (src, dst) in enumerate(
             (
                 (shift_hbm, shift), (index_hbm, index_ref), (weight_hbm, weight_ref), (x_hbm, xs),
-                (contact_hbm, contact), (kernel_hbm.at[4], middle_ref.at[0]),
-                (kernel_hbm.at[3], sides_ref.at[0]), (kernel_hbm.at[5], sides_ref.at[1]),
+                (contact_hbm, contact),
             )
         )
     ]
@@ -128,18 +127,6 @@
             form[0, at, :] = d[:LANES]
             form[1, at, :] = d[LANES:]
 
-        copies = [
-            pltpu.make_async_copy(
-                form.at[k, pl.ds(inside, tile)],
-                (other_hbm if flip else mine_hbm).at[k, pl.ds(inside, tile)],
-                form_sem.at[t, k],
-            )
-            for k in range(2)
-        ]
-        for c in copies:
-            c.start()
-        return copies
-
     def multiply(t):
         flip, inside, first, pair = steps[t]
         form = form_other if flip else form_mine
@@ -173,18 +160,18 @@
 
     count = len(steps)
     angles(0)
-    stores = unmix(0)
+    unmix(0)
     small[3].wait()
     for t in range(count):
         if t + 1 < count:
-            stores += unmix(t + 1)
+            unmix(t + 1)
         multiply(t)
         if t + 1 < count:
             angles(t + 1)
         if t > 0:
             add(t - 1)
     add(count - 1)
-    for c in small[4:] + stores:
+    for c in small[4:]:
         c.wait()
     cols = shift.shape[2]
     for o in range(mask_ref.shape[0]):
@@ -197,21 +184,21 @@
     return [pltpu.with_memory_space_constraint(a, pltpu.MemorySpace.HBM) for a in arrays]
 
 
-def project(x, shift, index, weight, contact, wave_form, near_kernel, row_mod, col_mod, scale, tile=TILE):
+def project(x, shift, index, weight, contact, wave_form, row_mod, col_mod, scale, tile=TILE):
     waves, _, width = wave_form.shape
     n = shift.shape[0] * shift.shape[2]
     sources = x.shape[0] // n
     half = pltpu.VMEM((waves // 2 // LANES, 2, sources, LANES), F32)
 
-    form = pltpu.HBM((2, waves // 2, width), BF16)
+    form = pltpu.VMEM((2, waves // 2, width), BF16)
 
     def body(*refs):
         project_body(*refs, tile=tile, row_mod=row_mod, col_mod=col_mod, scale=scale)
 
     return pl.pallas_call(
         body,
-        in_specs=[HBM] * 7,
-        out_specs=[VMEM] * 2 + [HBM] * 2 + [VMEM] * 5,
+        in_specs=[HBM] * 6,
+        out_specs=[VMEM] * 7,
         out_shape=[
             half,
             half,
@@ -220,13 +207,8 @@
             pltpu.VMEM((2, n, waves), F32),
             pltpu.VMEM(x.shape, BF16),
             pltpu.VMEM((contact.shape[2], n, LANES), F32),
-            pltpu.VMEM((1,) + near_kernel.shape[1:], BF16),
-            pltpu.VMEM((2,) + near_kernel.shape[1:], BF16),
         ],
         scratch_shapes=[
-            pltpu.VMEM((2, waves // 2, width), BF16),
-            pltpu.VMEM((2, waves // 2, width), BF16),
-            pltpu.SemaphoreType.DMA((waves // tile, 2)),
             pltpu.VMEM((2, x.shape[0], 2 * tile), F32),
             pltpu.SMEM(contact.shape, jnp.int32),
             pltpu.SMEM(shift.shape, jnp.int32),
@@ -239,7 +221,7 @@
         compiler_params=params(24),
         cost_estimate=cost(8 * x.shape[0] * width * waves, 5 << 20),
         name="project",
-    )(*in_hbm(x, shift, index, weight, contact, wave_form, near_kernel))
+    )(*in_hbm(x, shift, index, weight, contact, wave_form))
 
 
 def spread_body(trig_ref, form_ref, coeff_ref, base_ref, out_ref, lhs, *, flip, tile):
@@ -282,10 +264,12 @@
     )(trig, form, coeff, base)
 
 
-def near_body(*refs, offsets, coming, halo, after):
+def near_body(*refs, offsets, coming, halo, given, after):
     mask_ref, x = refs[:2]
     halos = refs[2 : 2 + halo]
-    held, refs = refs[2 + halo], refs[3 + halo :]
+    refs = refs[2 + halo :]
+    if given:
+        held, refs = refs[0], refs[1:]
     if coming:
         kernel_hbm, refs = refs[0], refs[1:]
     if after:
@@ -296,12 +280,16 @@
         copies = [
             pltpu.make_async_copy(kernel_hbm.at[o], refs[0].at[k], refs[2].at[k]) for k, o in enumerate(coming)
         ]
-        for c in copies:
-            c.start()
         refs = refs[1:]
     lhs = refs[0]
+    if not given:
+        held = refs[2]
+        own = pltpu.make_async_copy(kernel_hbm.at[offsets[0]], held.at[0], refs[3])
+        own.start()
+    for c in copies:
+        c.start()
     rows, cols, sources, full = x.shape
-    classes = held.shape[1]
+    classes = 2
 
     def block(r, c):
         if r < 0:
@@ -327,6 +315,8 @@
 
     for k, o in enumerate(offsets):
         gather(k)
+        if not given:
+            own.wait()
         upper, lower = [], []
         for v in range(classes):
             re, im = held[k, v, 0], held[k, v, 1]
@@ -351,9 +341,9 @@
     after = base is not None
 
     def body(*refs):
-        near_body(*refs, offsets=offsets, coming=coming, halo=len(halos), after=after)
-
-    operands = [mask, x, *halos, held]
+        near_body(*refs, offsets=offsets, coming=coming, halo=len(halos), given=held is not None, after=after)
+
+    operands = [mask, x, *halos] + ([] if held is None else [held])
     specs = [VMEM] * len(operands)
     out = [pltpu.VMEM((m, full), F32)]
     scratch = [pltpu.VMEM((2, m, classes * full), BF16)]
@@ -362,6 +352,8 @@
         specs += [HBM]
         out += [pltpu.VMEM((len(coming),) + kernel.shape[1:], BF16)]
         scratch += [pltpu.SemaphoreType.DMA((len(coming),))]
+    if held is None:
+        scratch += [pltpu.VMEM((1,) + kernel.shape[1:], BF16), pltpu.SemaphoreType.DMA(())]
     return pl.pallas_call(
         body,
         in_specs=specs + [VMEM] * after,
@@ -429,8 +421,8 @@
     shift = jnp.swapaxes(pillar_shift, 1, 2)
     index = wave_index.T
     weight = wave_weight.reshape(1, -1)
-    mine, other, form, form_other, trig, cells, mask, middle, sides = project(
-        field.reshape(-1, full), shift, index, weight, contact, wave_form, near_kernel, row_mod, col_mod, scale
+    mine, other, form, form_other, trig, cells, mask = project(
+        field.reshape(-1, full), shift, index, weight, contact, wave_form, row_mod, col_mod, scale
     )
     cells = cells.reshape(field.shape)
     total = mine + exchange(other, ((1, 0), (1, 0)))
@@ -449,7 +441,7 @@
     got = exchange(payload, steps[1])
     first, _, sort = paired(here[:, :1], here[:, cols - 1 :], "col")
     inner = first()
-    out, upper = near_field((4,), (0, 1, 2), mask, here, (), middle, near_kernel)
+    out, sides = near_field((4,), (3, 5), mask, here, (), None, near_kernel)
     total = total + unpack(got)
 
     west, east = sort(inner, outer)
@@ -459,14 +451,13 @@
     high = jnp.concatenate([west[-1:], cells[-1:], east[-1:]], axis=1)
     first, second, sort = paired(low, high, "row")
     north, south = sort(first(), second())
-    out, lower = near_field((3, 5), (6, 7, 8), mask, cells, (west, east), sides, near_kernel, out)
+    out, outer_held = near_field((3, 5), (0, 1, 2, 6, 7, 8), mask, cells, (west, east), sides, near_kernel, out)
     total = total + unpack(got)
 
     payload, out = tie((pack(total), out))
     got = exchange(payload, steps[3])
     halos = (west, east, north, south)
-    (out,) = near_field((0, 1, 2), (), mask, cells, halos, upper, near_kernel, out)
-    (out,) = near_field((6, 7, 8), (), mask, cells, halos, lower, near_kernel, out)
+    (out,) = near_field((0, 1, 2, 6, 7, 8), (), mask, cells, halos, outer_held, near_kernel, out)
     total = total + unpack(got)
     for dims in steps[4:]:
         total = total + unpack(exchange(pack(total), dims))

time: 37 us -> 37 us (level)
  other arithmetic: 0.88 us -> 1.83 us
  waiting for transfers between devices: 2.65 us -> 1.98 us
    convert_element_type x4, other arithmetic: 0.55 us -> 1.5 us  [pack(): (value * (128.0 * lax.rsqrt(jnp.maximum(jnp.abs(value), 1e-36)))).astype(...]
    pallas_call x1, Pallas kernels: 5.88 us -> 5 us  [project(): pl.pallas_call(body, in_specs=[HBM] * 6, out_specs=[VMEM] * 7, out_shape=...]
    pallas_call x4 -> x3, Pallas kernels: 7.52 us -> 8.1 us  [near_field(): pl.pallas_call(body, in_specs=specs + [VMEM] * after, out_specs=[VMEM] *...]
    ppermute x2, waiting for transfers between devices: 0.98 us -> 0.59 us  [second(): return lax.ppermute(jnp.where(odd, high, low), axis, outer)]
  transfers between devices with their start and end apart: 10 -> 10, of which waited for: 5 -> 3; matrix products, arithmetic and copies ran while one was open for 2% -> 2% of each run, Pallas kernels for 24% -> 25%
where the time goes in v3:
time: 37 us; the launch traced here: 36.8 us
  Pallas kernels  16.6 us (45%)
  starting transfers between devices  16.2 us (44%)
  waiting for transfers between devices  1.98 us (5%)
  other arithmetic  1.83 us (5%)
    ppermute x6, starting transfers between devices, exchange(): return lax.ppermute(value, ('row', 'col'), pairs)  9.45 us
    pallas_call x3, Pallas kernels, near_field(): pl.pallas_call(body, in_specs=specs + [VMEM] * after, out_specs=[VMEM] *...  8.1 us
    pallas_call x1, Pallas kernels, project(): pl.pallas_call(body, in_specs=[HBM] * 6, out_specs=[VMEM] * 7, out_shape=...  5 us
    ppermute x2, starting transfers between devices, second(): return lax.ppermute(jnp.where(odd, high, low), axis, outer)  4.94 us
    pallas_call x2, Pallas kernels, spread(): pl.pallas_call(body, in_specs=[VMEM] * 4, out_specs=VMEM, out_shape=jax.S...  3.49 us
    ppermute x2, starting transfers between devices, first(): return lax.ppermute(jnp.where(odd, low, high), axis, inner)  1.82 us
    convert_element_type x4, other arithmetic, pack(): (value * (128.0 * lax.rsqrt(jnp.maximum(jnp.abs(value), 1e-36)))).astype(...  1.5 us
    ppermute x6, waiting for transfers between devices, exchange(): return lax.ppermute(value, ('row', 'col'), pairs)  1.38 us
  transfers between devices with their start and end apart: 10, of which 3 were waited for; matrix products, arithmetic and copies ran while one was open for 2% of the time, Pallas kernels for 25%

profile of v3, /device:TPU:0, one launch (start us, length us, event | category | flops | bytes accessed | tf_op | source)
XLA Modules:
  0.0 36.8 jit_solution(8830525045680744599)
XLA Ops:
  0.0 5.0 %project.1 = (f32[8,2,32,128]{3,2,1,0:T(8,128)S(1)}, f32[8,2,32,128]{3,2,1,0:T(8,128)S(1)}, bf16[2,1024,256]{2,1,0:T(8,128)(2,1)S(1)}, bf16[2,1024,256]{2,1,0:T(...) custom-call(bf16[512,512]{1,0:T(8,128)(2,1)} %bitcast.15, ...), custom_call_target="tpu_custom_call" | custom-call | flops 2147483648 | bytes 5242880 | tf_op jit(solution)/shard_map/project/pallas_call | solution.py:198
  5.0 0.5 %collective-permute-start = (f32[8,2,32,128]{3,2,1,0:T(8,128)S(1)}, f32[8,2,32,128]{3,2,1,0:T(8,128)}, u32[]{:S(2)}, u32[]{:S(2)}) collective-permute-start(f32[8,2,32,128]{3,2,1,0:T(8,128)S(1)} %get-tuple-element.29), channel_id=1, source_target_pairs={{0,4},{1,5},{2,6},{3,7},{4,0},{5,1},{6,2},{7,3},{8,12},{9,13},{10,... | collective-permute-start | bytes 786440 | tf_op jit(solution)/shard_map/ppermute | solution.py:402
  5.5 1.3 %collective-permute-done = f32[8,2,32,128]{3,2,1,0:T(8,128)} collective-permute-done((f32[8,2,32,128]{3,2,1,0:T(8,128)S(1)}, f32[8,2,32,128]{3,2,1,0:T(8,128)}, u32[]{:S(2)}, u32[]{:S(2)}) %collective-permute-start) | collective-permute-done | bytes 262176 | tf_op jit(solution)/shard_map/ppermute | solution.py:402
  6.8 1.0 %multiply_convert_fusion.3 = (f16[8,2,32,128]{3,2,1,0:T(8,128)(2,1)S(1)}, f32[8,2,32,128]{3,2,1,0:T(8,128)S(1)}) fusion(f32[8,2,32,128]{3,2,1,0:T(8,128)S(1)} %get-tuple-element.28, f32[8,2,32,128]{3,2,1,0:T(8,128)} %collective-permute-done), kind=kLoop, calls=%fused_computation.16 | loop fusion | flops 393216 | bytes 917504 | tf_op jit(solution)/shard_map/convert_element_type | solution.py:406
  7.8 2.9 %collective-permute-start.1 = (f16[8,2,32,128]{3,2,1,0:T(8,128)(2,1)S(1)}, f16[8,2,32,128]{3,2,1,0:T(8,128)(2,1)S(1)}, u32[]{:S(2)}, u32[]{:S(2)}) collective-permute-start(f16[8,2,32,128]{3,2,1,0:T(8,128)(2,1)S(1)} %get-tuple-element.31), channel_id=1, source_target_pairs={{0,8},{1,9},{2,10},{3,11},{4,20},{5,21},{6,22},{7,23},{8,0},{9,1},... | collective-permute-start | bytes 393224 | tf_op jit(solution)/shard_map/ppermute | solution.py:402
  10.8 3.7 %collective-permute-start.5 = (bf16[4,1,32,512]{3,2,1,0:T(8,128)(2,1)S(1)}, bf16[4,1,32,512]{3,2,1,0:T(8,128)(2,1)S(1)}, u32[]{:S(2)}, u32[]{:S(2)}) collective-permute-start(bf16[4,1,32,512]{3,2,1,0:T(8,128)(2,1)S(1)} %slice_select_fusion), channel_id=1, source_target_pairs={{0,3},{1,2},{2,1},{3,0},{4,7},{5,6},{6,5},{7,4},{8,11},{9,10},{10,... | collective-permute-start | bytes 393224 | tf_op jit(solution)/shard_map/ppermute | solution.py:379
  14.5 0.0 collective-permute-done.1
  14.5 0.1 multiply_convert_fusion.2
  14.6 1.6 %collective-permute-start.2 = (f16[8,2,32,128]{3,2,1,0:T(8,128)(2,1)S(1)}, f16[8,2,32,128]{3,2,1,0:T(8,128)(2,1)S(1)}, u32[]{:S(2)}, u32[]{:S(2)}) collective-permute-start(f16[8,2,32,128]{3,2,1,0:T(8,128)(2,1)S(1)} %multiply_convert_fusion.2), channel_id=1, source_target_pairs={{0,16},{1,17},{2,18},{3,19},{4,12},{5,13},{6,14},{7,15},{8,24},{9,... | collective-permute-start | bytes 393224 | tf_op jit(solution)/shard_map/ppermute | solution.py:402
  16.2 1.4 %collective-permute-start.4 = (bf16[4,1,32,512]{3,2,1,0:T(8,128)(2,1)S(1)}, bf16[4,1,32,512]{3,2,1,0:T(8,128)(2,1)S(1)}, u32[]{:S(2)}, u32[]{:S(2)}) collective-permute-start(bf16[4,1,32,512]{3,2,1,0:T(8,128)(2,1)S(1)} %slice_select_fusion.1), channel_id=1, source_target_pairs={{0,1},{1,0},{2,3},{3,2},{4,5},{5,4},{6,7},{7,6},{8,9},{9,8},{10,11... | collective-permute-start | bytes 393224 | tf_op jit(solution)/shard_map/ppermute | solution.py:376
  17.6 2.0 %near.3 = (f32[512,512]{1,0:T(8,128)S(1)}, bf16[2,2,2,256,256]{4,3,2,1,0:T(8,128)(2,1)S(1)}) custom-call(f32[9,16,128]{2,1,0:T(8,128)S(1)} %get-tuple-element.34.refs_0_, bf16[4,4,32,512]{3,2,1,0:T(8,128)(2,1)S(1)} %bitcast.10, bf16[9,2,2,256,256]{4,3,2,1,0:T(8,128)(2,1)} %refs_5_.3), custom_call_target="tpu_custom_call" | custom-call | flops 536870912 | bytes 4194304 | tf_op jit(solution)/shard_map/near/pallas_call | solution.py:357
  19.6 0.0 collective-permute-done.2
  19.6 0.2 multiply_convert_fusion.1
  19.8 1.4 %collective-permute-start.3 = (f16[8,2,32,128]{3,2,1,0:T(8,128)(2,1)S(1)}, f16[8,2,32,128]{3,2,1,0:T(8,128)(2,1)S(1)}, u32[]{:S(2)}, u32[]{:S(2)}) collective-permute-start(f16[8,2,32,128]{3,2,1,0:T(8,128)(2,1)S(1)} %multiply_convert_fusion.1), channel_id=1, source_target_pairs={{0,1},{1,0},{2,3},{3,2},{4,6},{5,7},{6,4},{7,5},{8,9},{9,8},{10,11... | collective-permute-start | bytes 393224 | tf_op jit(solution)/shard_map/ppermute | solution.py:402
  21.2 0.0 collective-permute-done.5
  21.2 0.0 collective-permute-done.4
  21.3 0.1 broadcast_select_fusion.2
  21.3 1.3 %collective-permute-start.8 = (bf16[1,6,32,512]{3,2,1,0:T(8,128)(2,1)S(1)}, bf16[1,6,32,512]{3,2,1,0:T(8,128)(2,1)S(1)}, u32[]{:S(2)}, u32[]{:S(2)}) collective-permute-start(bf16[1,6,32,512]{3,2,1,0:T(8,128)(2,1)S(1)} %get-tuple-element.53), channel_id=1, source_target_pairs={{0,28},{4,8},{8,4},{12,16},{16,12},{20,24},{24,20},{28,0},{1,29},{... | collective-permute-start | bytes 589832 | tf_op jit(solution)/shard_map/ppermute | solution.py:379
  22.6 0.4 %collective-permute-start.7 = (bf16[1,6,32,512]{3,2,1,0:T(8,128)(2,1)S(1)}, bf16[1,6,32,512]{3,2,1,0:T(8,128)(2,1)S(1)}, u32[]{:S(2)}, u32[]{:S(2)}) collective-permute-start(bf16[1,6,32,512]{3,2,1,0:T(8,128)(2,1)S(1)} %get-tuple-element.54), channel_id=1, source_target_pairs={{0,4},{4,0},{8,12},{12,8},{16,20},{20,16},{24,28},{28,24},{1,5},{5... | collective-permute-start | bytes 589832 | tf_op jit(solution)/shard_map/ppermute | solution.py:376
  23.0 2.7 %near.4 = (f32[512,512]{1,0:T(8,128)S(1)}, bf16[6,2,2,256,256]{4,3,2,1,0:T(8,128)(2,1)S(1)}) custom-call(f32[9,16,128]{2,1,0:T(8,128)S(1)} %get-tuple-element.34.refs_0_, bf16[4,4,32,512]{3,2,1,0:T(8,128)(2,1)S(1)} %bitcast.11, bf16[4,1,32,512]{3,2,1,0:T(8,128)(2,1)S(1)} %get-tuple-element.56.refs_2_, bf16[4,1,32,512]{3,2,1,0:T(8,128)(2,1)S(1)} %get-tuple-element.55.refs_3_, ...), custom_call_target="tpu_custom_call" | custom-call | flops 1073741824 | bytes 4194304 | tf_op jit(solution)/shard_map/near/pallas_call | solution.py:357
  25.7 0.0 collective-permute-done.3
  25.7 0.2 multiply_convert_fusion
  25.9 2.9 %collective-permute-start.6 = (f16[8,2,32,128]{3,2,1,0:T(8,128)(2,1)S(1)}, f16[8,2,32,128]{3,2,1,0:T(8,128)(2,1)S(1)}, u32[]{:S(2)}, u32[]{:S(2)}) collective-permute-start(f16[8,2,32,128]{3,2,1,0:T(8,128)(2,1)S(1)} %multiply_convert_fusion), channel_id=1, source_target_pairs={{0,2},{1,3},{2,0},{3,1},{4,5},{5,4},{6,7},{7,6},{8,10},{9,11},{10,... | collective-permute-start | bytes 393224 | tf_op jit(solution)/shard_map/ppermute | solution.py:402
  28.8 0.6 %collective-permute-done.8 = bf16[1,6,32,512]{3,2,1,0:T(8,128)(2,1)S(1)} collective-permute-done((bf16[1,6,32,512]{3,2,1,0:T(8,128)(2,1)S(1)}, bf16[1,6,32,512]{3,2,1,0:T(8,128)(2,1)S(1)}, u32[]{:S(2)}, u32[]{:S(2)}) %collective-permute-start.8) | collective-permute-done | bytes 196640 | tf_op jit(solution)/shard_map/ppermute | solution.py:379
  29.4 0.0 collective-permute-done.7
  29.4 3.5 %near.5.refs_3_ = f32[512,512]{1,0:T(8,128)S(1)} custom-call(f32[9,16,128]{2,1,0:T(8,128)S(1)} %get-tuple-element.34.refs_0_, bf16[4,4,32,512]{3,2,1,0:T(8,128)(2,1)S(1)} %bitcast.12, bf16[4,1,32,512]{3,2,1,0:T(8,128)(2,1)S(1)} %get-tuple-element.56.refs_2_, bf16[4,1,32,512]{3,2,1,0:T(8,128)(2,1)S(1)} %get-tuple-element.55.refs_3_, ...), custom_call_target="tpu_custom_call" | custom-call | flops 3221225472 | bytes 4194304 | tf_op jit(solution)/shard_map/near/pallas_call | solution.py:357
  32.9 0.0 collective-permute-done.6
  32.9 0.2 fusion.8.refs_2_
  33.1 0.1 collective-permute-start.9
  33.2 1.3 %spread.2.refs_3_ = f32[512,512]{1,0:T(8,128)S(1)} custom-call(f32[2,16,2048]{2,1,0:T(8,128)S(1)} %get-tuple-element.26.refs_0_, bf16[2,1024,256]{2,1,0:T(8,128)(2,1)S(1)} %get-tuple-element.45.refs_1_, bf16[8,2,32,128]{3,2,1,0:T(8,128)(2,1)S(1)} %fusion.8.refs_2_, f32[512,512]{1,0:T(8,128)S(1)} %near.5.refs_3_), custom_call_target="tpu_custom_call" | custom-call | flops 1073741824 | bytes 5242880 | tf_op jit(solution)/shard_map/spread/pallas_call | solution.py:255
  34.5 0.1 collective-permute-done.9.refs_2_
  34.5 2.2 %spread.3 = f32[512,512]{1,0:T(8,128)} custom-call(f32[2,16,2048]{2,1,0:T(8,128)S(1)} %get-tuple-element.26.refs_0_, bf16[2,1024,256]{2,1,0:T(8,128)(2,1)S(1)} %get-tuple-element.27.refs_1_, bf16[8,2,32,128]{3,2,1,0:T(8,128)(2,1)S(1)} %collective-permute-done.9.refs_2_, f32[512,512]{1,0:T(8,128)S(1)} %spread.2.refs_3_), custom_call_target="tpu_custom_call" | custom-call | flops 1073741824 | bytes 5242880 | tf_op jit(solution)/shard_map/spread/pallas_call | solution.py:255
  (6 shorter events, 0.1 us)
Async XLA Ops:
  5.0 1.8 %collective-permute-start = (f32[8,2,32,128]{3,2,1,0:T(8,128)S(1)}, f32[8,2,32,128]{3,2,1,0:T(8,128)}, u32[]{:S(2)}, u32[]{:S(2)}) collective-permute-start(f32[8,2,32,128]{3,2,1,0:T(8,128)S(1)} %get-tuple-element.29), channel_id=1, source_target_pairs={{0,4},{1,5},{2,6},{3,7},{4,0},{5,1},{6,2},{7,3},{8,12},{9,13},{10,... | collective-permute-start | bytes 786440 | tf_op jit(solution)/shard_map/ppermute | solution.py:402
  7.8 6.6 %collective-permute-start.1 = (f16[8,2,32,128]{3,2,1,0:T(8,128)(2,1)S(1)}, f16[8,2,32,128]{3,2,1,0:T(8,128)(2,1)S(1)}, u32[]{:S(2)}, u32[]{:S(2)}) collective-permute-start(f16[8,2,32,128]{3,2,1,0:T(8,128)(2,1)S(1)} %get-tuple-element.31), channel_id=1, source_target_pairs={{0,8},{1,9},{2,10},{3,11},{4,20},{5,21},{6,22},{7,23},{8,0},{9,1},... | collective-permute-start | bytes 393224 | tf_op jit(solution)/shard_map/ppermute | solution.py:402
  10.8 10.4 %collective-permute-start.5 = (bf16[4,1,32,512]{3,2,1,0:T(8,128)(2,1)S(1)}, bf16[4,1,32,512]{3,2,1,0:T(8,128)(2,1)S(1)}, u32[]{:S(2)}, u32[]{:S(2)}) collective-permute-start(bf16[4,1,32,512]{3,2,1,0:T(8,128)(2,1)S(1)} %slice_select_fusion), channel_id=1, source_target_pairs={{0,3},{1,2},{2,1},{3,0},{4,7},{5,6},{6,5},{7,4},{8,11},{9,10},{10,... | collective-permute-start | bytes 393224 | tf_op jit(solution)/shard_map/ppermute | solution.py:379
  14.6 5.0 %collective-permute-start.2 = (f16[8,2,32,128]{3,2,1,0:T(8,128)(2,1)S(1)}, f16[8,2,32,128]{3,2,1,0:T(8,128)(2,1)S(1)}, u32[]{:S(2)}, u32[]{:S(2)}) collective-permute-start(f16[8,2,32,128]{3,2,1,0:T(8,128)(2,1)S(1)} %multiply_convert_fusion.2), channel_id=1, source_target_pairs={{0,16},{1,17},{2,18},{3,19},{4,12},{5,13},{6,14},{7,15},{8,24},{9,... | collective-permute-start | bytes 393224 | tf_op jit(solution)/shard_map/ppermute | solution.py:402
  16.2 5.0 %collective-permute-start.4 = (bf16[4,1,32,512]{3,2,1,0:T(8,128)(2,1)S(1)}, bf16[4,1,32,512]{3,2,1,0:T(8,128)(2,1)S(1)}, u32[]{:S(2)}, u32[]{:S(2)}) collective-permute-start(bf16[4,1,32,512]{3,2,1,0:T(8,128)(2,1)S(1)} %slice_select_fusion.1), channel_id=1, source_target_pairs={{0,1},{1,0},{2,3},{3,2},{4,5},{5,4},{6,7},{7,6},{8,9},{9,8},{10,11... | collective-permute-start | bytes 393224 | tf_op jit(solution)/shard_map/ppermute | solution.py:376
  19.8 5.9 %collective-permute-start.3 = (f16[8,2,32,128]{3,2,1,0:T(8,128)(2,1)S(1)}, f16[8,2,32,128]{3,2,1,0:T(8,128)(2,1)S(1)}, u32[]{:S(2)}, u32[]{:S(2)}) collective-permute-start(f16[8,2,32,128]{3,2,1,0:T(8,128)(2,1)S(1)} %multiply_convert_fusion.1), channel_id=1, source_target_pairs={{0,1},{1,0},{2,3},{3,2},{4,6},{5,7},{6,4},{7,5},{8,9},{9,8},{10,11... | collective-permute-start | bytes 393224 | tf_op jit(solution)/shard_map/ppermute | solution.py:402
  21.3 8.1 %collective-permute-start.8 = (bf16[1,6,32,512]{3,2,1,0:T(8,128)(2,1)S(1)}, bf16[1,6,32,512]{3,2,1,0:T(8,128)(2,1)S(1)}, u32[]{:S(2)}, u32[]{:S(2)}) collective-permute-start(bf16[1,6,32,512]{3,2,1,0:T(8,128)(2,1)S(1)} %get-tuple-element.53), channel_id=1, source_target_pairs={{0,28},{4,8},{8,4},{12,16},{16,12},{20,24},{24,20},{28,0},{1,29},{... | collective-permute-start | bytes 589832 | tf_op jit(solution)/shard_map/ppermute | solution.py:379
  22.6 6.8 %collective-permute-start.7 = (bf16[1,6,32,512]{3,2,1,0:T(8,128)(2,1)S(1)}, bf16[1,6,32,512]{3,2,1,0:T(8,128)(2,1)S(1)}, u32[]{:S(2)}, u32[]{:S(2)}) collective-permute-start(bf16[1,6,32,512]{3,2,1,0:T(8,128)(2,1)S(1)} %get-tuple-element.54), channel_id=1, source_target_pairs={{0,4},{4,0},{8,12},{12,8},{16,20},{20,16},{24,28},{28,24},{1,5},{5... | collective-permute-start | bytes 589832 | tf_op jit(solution)/shard_map/ppermute | solution.py:376
  25.9 7.0 %collective-permute-start.6 = (f16[8,2,32,128]{3,2,1,0:T(8,128)(2,1)S(1)}, f16[8,2,32,128]{3,2,1,0:T(8,128)(2,1)S(1)}, u32[]{:S(2)}, u32[]{:S(2)}) collective-permute-start(f16[8,2,32,128]{3,2,1,0:T(8,128)(2,1)S(1)} %multiply_convert_fusion), channel_id=1, source_target_pairs={{0,2},{1,3},{2,0},{3,1},{4,5},{5,4},{6,7},{7,6},{8,10},{9,11},{10,... | collective-permute-start | bytes 393224 | tf_op jit(solution)/shard_map/ppermute | solution.py:402
  33.1 1.4 %collective-permute-start.9 = (bf16[8,2,32,128]{3,2,1,0:T(8,128)(2,1)S(1)}, bf16[8,2,32,128]{3,2,1,0:T(8,128)(2,1)S(1)}, u32[]{:S(2)}, u32[]{:S(2)}) collective-permute-start(bf16[8,2,32,128]{3,2,1,0:T(8,128)(2,1)S(1)} %fusion.8.refs_2_), channel_id=1, source_target_pairs={{0,4},{1,5},{2,6},{3,7},{4,0},{5,1},{6,2},{7,3},{8,12},{9,13},{10,... | collective-permute-start | bytes 393224 | tf_op jit(solution)/shard_map/ppermute | solution.py:402

commit v4 on v2

--- a/solution.py
+++ b/solution.py
@@ -449,7 +449,7 @@
     got = exchange(payload, steps[1])
     first, _, sort = paired(here[:, :1], here[:, cols - 1 :], "col")
     inner = first()
-    out, upper = near_field((4,), (0, 1, 2), mask, here, (), middle, near_kernel)
+    out, outer_held = near_field((4,), (0, 1, 2, 6, 7, 8), mask, here, (), middle, near_kernel)
     total = total + unpack(got)
 
     west, east = sort(inner, outer)
@@ -459,14 +459,13 @@
     high = jnp.concatenate([west[-1:], cells[-1:], east[-1:]], axis=1)
     first, second, sort = paired(low, high, "row")
     north, south = sort(first(), second())
-    out, lower = near_field((3, 5), (6, 7, 8), mask, cells, (west, east), sides, near_kernel, out)
+    (out,) = near_field((3, 5), (), mask, cells, (west, east), sides, near_kernel, out)
     total = total + unpack(got)
 
     payload, out = tie((pack(total), out))
     got = exchange(payload, steps[3])
     halos = (west, east, north, south)
-    (out,) = near_field((0, 1, 2), (), mask, cells, halos, upper, near_kernel, out)
-    (out,) = near_field((6, 7, 8), (), mask, cells, halos, lower, near_kernel, out)
+    (out,) = near_field((0, 1, 2, 6, 7, 8), (), mask, cells, halos, outer_held, near_kernel, out)
     total = total + unpack(got)
     for dims in steps[4:]:
         total = total + unpack(exchange(pack(total), dims))

time: 37 us -> 36.8 us (level)
  waiting for transfers between devices: 2.65 us -> 3.97 us
  starting transfers between devices: 16.2 us -> 15.4 us
  Pallas kernels: 16.9 us -> 16.1 us
    pallas_call x4 -> x3, Pallas kernels: 7.52 us -> 6.73 us  [near_field(): pl.pallas_call(body, in_specs=specs + [VMEM] * after, out_specs=[VMEM] *...]
    ppermute x6, starting transfers between devices: 9.42 us -> 8.66 us  [exchange(): return lax.ppermute(value, ('row', 'col'), pairs)]
    ppermute x2, waiting for transfers between devices: 0.98 us -> 1.71 us  [second(): return lax.ppermute(jnp.where(odd, high, low), axis, outer)]
    ppermute x6, waiting for transfers between devices: 1.65 us -> 2.25 us  [exchange(): return lax.ppermute(value, ('row', 'col'), pairs)]
  transfers between devices with their start and end apart: 10 -> 10, of which waited for: 5 -> 4; matrix products, arithmetic and copies ran while one was open for 2% -> 2% of each run, Pallas kernels for 24% -> 22%
where the time goes in v4:
time: 36.8 us; the launch traced here: 36.6 us
  Pallas kernels  16.1 us (44%)
  starting transfers between devices  15.4 us (42%)
  waiting for transfers between devices  3.97 us (11%)
  other arithmetic  0.89 us (2%)
    ppermute x6, starting transfers between devices, exchange(): return lax.ppermute(value, ('row', 'col'), pairs)  8.66 us
    pallas_call x3, Pallas kernels, near_field(): pl.pallas_call(body, in_specs=specs + [VMEM] * after, out_specs=[VMEM] *...  6.73 us
    pallas_call x1, Pallas kernels, project(): pl.pallas_call(body, in_specs=[HBM] * 7, out_specs=[VMEM] * 2 + [HBM] * 2...  5.88 us
    ppermute x2, starting transfers between devices, second(): return lax.ppermute(jnp.where(odd, high, low), axis, outer)  4.94 us
    pallas_call x2, Pallas kernels, spread(): pl.pallas_call(body, in_specs=[VMEM] * 4, out_specs=VMEM, out_shape=jax.S...  3.49 us
    ppermute x6, waiting for transfers between devices, exchange(): return lax.ppermute(value, ('row', 'col'), pairs)  2.25 us
    ppermute x2, starting transfers between devices, first(): return lax.ppermute(jnp.where(odd, low, high), axis, inner)  1.82 us
    ppermute x2, waiting for transfers between devices, second(): return lax.ppermute(jnp.where(odd, high, low), axis, outer)  1.71 us
  transfers between devices with their start and end apart: 10, of which 4 were waited for; matrix products, arithmetic and copies ran while one was open for 2% of the time, Pallas kernels for 22%

profile of v4, /device:TPU:0, one launch (start us, length us, event | category | flops | bytes accessed | tf_op | source)
XLA Modules:
  0.0 36.6 jit_solution(13653417164570118607)
XLA Ops:
  0.0 5.9 %project.1 = (f32[8,2,32,128]{3,2,1,0:T(8,128)S(1)}, f32[8,2,32,128]{3,2,1,0:T(8,128)S(1)}, bf16[2,1024,256]{2,1,0:T(8,128)(2,1)}, bf16[2,1024,256]{2,1,0:T(8,12...) custom-call(bf16[512,512]{1,0:T(8,128)(2,1)} %bitcast.15, ...), custom_call_target="tpu_custom_call" | custom-call | flops 2147483648 | bytes 5242880 | tf_op jit(solution)/shard_map/project/pallas_call | solution.py:211
  5.9 0.5 %collective-permute-start = (f32[8,2,32,128]{3,2,1,0:T(8,128)S(1)}, f32[8,2,32,128]{3,2,1,0:T(8,128)S(1)}, u32[]{:S(2)}, u32[]{:S(2)}) collective-permute-start(f32[8,2,32,128]{3,2,1,0:T(8,128)S(1)} %get-tuple-element.29), channel_id=1, source_target_pairs={{0,4},{1,5},{2,6},{3,7},{4,0},{5,1},{6,2},{7,3},{8,12},{9,13},{10,... | collective-permute-start | bytes 786440 | tf_op jit(solution)/shard_map/ppermute | solution.py:410
  6.4 1.1 %collective-permute-done = f32[8,2,32,128]{3,2,1,0:T(8,128)S(1)} collective-permute-done((f32[8,2,32,128]{3,2,1,0:T(8,128)S(1)}, f32[8,2,32,128]{3,2,1,0:T(8,128)S(1)}, u32[]{:S(2)}, u32[]{:S(2)}) %collective-permute-start) | collective-permute-done | bytes 262176 | tf_op jit(solution)/shard_map/ppermute | solution.py:410
  7.6 0.1 multiply_convert_fusion.3
  7.7 2.9 %collective-permute-start.1 = (f16[8,2,32,128]{3,2,1,0:T(8,128)(2,1)S(1)}, f16[8,2,32,128]{3,2,1,0:T(8,128)(2,1)S(1)}, u32[]{:S(2)}, u32[]{:S(2)}) collective-permute-start(f16[8,2,32,128]{3,2,1,0:T(8,128)(2,1)S(1)} %get-tuple-element.31), channel_id=1, source_target_pairs={{0,8},{1,9},{2,10},{3,11},{4,20},{5,21},{6,22},{7,23},{8,0},{9,1},... | collective-permute-start | bytes 393224 | tf_op jit(solution)/shard_map/ppermute | solution.py:410
  10.6 3.7 %collective-permute-start.5 = (bf16[4,1,32,512]{3,2,1,0:T(8,128)(2,1)S(1)}, bf16[4,1,32,512]{3,2,1,0:T(8,128)(2,1)S(1)}, u32[]{:S(2)}, u32[]{:S(2)}) collective-permute-start(bf16[4,1,32,512]{3,2,1,0:T(8,128)(2,1)S(1)} %slice_select_fusion), channel_id=1, source_target_pairs={{0,3},{1,2},{2,1},{3,0},{4,7},{5,6},{6,5},{7,4},{8,11},{9,10},{10,... | collective-permute-start | bytes 393224 | tf_op jit(solution)/shard_map/ppermute | solution.py:387
  14.3 0.0 collective-permute-done.1
  14.3 0.1 multiply_convert_fusion.2
  14.4 1.6 %collective-permute-start.2 = (f16[8,2,32,128]{3,2,1,0:T(8,128)(2,1)S(1)}, f16[8,2,32,128]{3,2,1,0:T(8,128)(2,1)S(1)}, u32[]{:S(2)}, u32[]{:S(2)}) collective-permute-start(f16[8,2,32,128]{3,2,1,0:T(8,128)(2,1)S(1)} %multiply_convert_fusion.2), channel_id=1, source_target_pairs={{0,16},{1,17},{2,18},{3,19},{4,12},{5,13},{6,14},{7,15},{8,24},{9,... | collective-permute-start | bytes 393224 | tf_op jit(solution)/shard_map/ppermute | solution.py:410
  16.0 1.4 %collective-permute-start.4 = (bf16[4,1,32,512]{3,2,1,0:T(8,128)(2,1)S(1)}, bf16[4,1,32,512]{3,2,1,0:T(8,128)(2,1)S(1)}, u32[]{:S(2)}, u32[]{:S(2)}) collective-permute-start(bf16[4,1,32,512]{3,2,1,0:T(8,128)(2,1)S(1)} %slice_select_fusion.1), channel_id=1, source_target_pairs={{0,1},{1,0},{2,3},{3,2},{4,5},{5,4},{6,7},{7,6},{8,9},{9,8},{10,11... | collective-permute-start | bytes 393224 | tf_op jit(solution)/shard_map/ppermute | solution.py:384
  17.4 2.0 %near.3 = (f32[512,512]{1,0:T(8,128)S(1)}, bf16[6,2,2,256,256]{4,3,2,1,0:T(8,128)(2,1)S(1)}) custom-call(f32[9,16,128]{2,1,0:T(8,128)S(1)} %get-tuple-element.34.refs_0_, bf16[4,4,32,512]{3,2,1,0:T(8,128)(2,1)S(1)} %bitcast.10, bf16[1,2,2,256,256]{4,3,2,1,0:T(8,128)(2,1)S(1)} %get-tuple-element.36.refs_2_, bf16[9,2,2,256,256]{4,3,2,1,0:T(8,128)(2,1)} %refs_3_.1), custom_call_target="tpu_custom_call" | custom-call | flops 536870912 | bytes 4194304 | tf_op jit(solution)/shard_map/near/pallas_call | solution.py:365
  19.4 0.0 collective-permute-done.2
  19.4 0.2 multiply_convert_fusion.1
  19.6 1.4 %collective-permute-start.3 = (f16[8,2,32,128]{3,2,1,0:T(8,128)(2,1)S(1)}, f16[8,2,32,128]{3,2,1,0:T(8,128)(2,1)S(1)}, u32[]{:S(2)}, u32[]{:S(2)}) collective-permute-start(f16[8,2,32,128]{3,2,1,0:T(8,128)(2,1)S(1)} %multiply_convert_fusion.1), channel_id=1, source_target_pairs={{0,1},{1,0},{2,3},{3,2},{4,6},{5,7},{6,4},{7,5},{8,9},{9,8},{10,11... | collective-permute-start | bytes 393224 | tf_op jit(solution)/shard_map/ppermute | solution.py:410
  21.0 0.0 collective-permute-done.5
  21.0 0.0 collective-permute-done.4
  21.1 0.1 broadcast_select_fusion.2
  21.1 1.3 %collective-permute-start.8 = (bf16[1,6,32,512]{3,2,1,0:T(8,128)(2,1)S(1)}, bf16[1,6,32,512]{3,2,1,0:T(8,128)(2,1)S(1)}, u32[]{:S(2)}, u32[]{:S(2)}) collective-permute-start(bf16[1,6,32,512]{3,2,1,0:T(8,128)(2,1)S(1)} %get-tuple-element.53), channel_id=1, source_target_pairs={{0,28},{4,8},{8,4},{12,16},{16,12},{20,24},{24,20},{28,0},{1,29},{... | collective-permute-start | bytes 589832 | tf_op jit(solution)/shard_map/ppermute | solution.py:387
  22.4 0.4 %collective-permute-start.7 = (bf16[1,6,32,512]{3,2,1,0:T(8,128)(2,1)S(1)}, bf16[1,6,32,512]{3,2,1,0:T(8,128)(2,1)S(1)}, u32[]{:S(2)}, u32[]{:S(2)}) collective-permute-start(bf16[1,6,32,512]{3,2,1,0:T(8,128)(2,1)S(1)} %get-tuple-element.54), channel_id=1, source_target_pairs={{0,4},{4,0},{8,12},{12,8},{16,20},{20,16},{24,28},{28,24},{1,5},{5... | collective-permute-start | bytes 589832 | tf_op jit(solution)/shard_map/ppermute | solution.py:384
  22.8 1.3 %near.4.refs_7_ = f32[512,512]{1,0:T(8,128)S(1)} custom-call(f32[9,16,128]{2,1,0:T(8,128)S(1)} %get-tuple-element.34.refs_0_, bf16[4,4,32,512]{3,2,1,0:T(8,128)(2,1)S(1)} %bitcast.11, bf16[4,1,32,512]{3,2,1,0:T(8,128)(2,1)S(1)} %get-tuple-element.56.refs_2_, bf16[4,1,32,512]{3,2,1,0:T(8,128)(2,1)S(1)} %get-tuple-element.55.refs_3_, ...), custom_call_target="tpu_custom_call" | custom-call | flops 1073741824 | bytes 4194304 | tf_op jit(solution)/shard_map/near/pallas_call | solution.py:365
  24.1 1.0 %collective-permute-done.3 = f16[8,2,32,128]{3,2,1,0:T(8,128)(2,1)S(1)} collective-permute-done((f16[8,2,32,128]{3,2,1,0:T(8,128)(2,1)S(1)}, f16[8,2,32,128]{3,2,1,0:T(8,128)(2,1)S(1)}, u32[]{:S(2)}, u32[]{:S(2)}) %collective-permute-start.3) | collective-permute-done | bytes 131104 | tf_op jit(solution)/shard_map/ppermute | solution.py:410
  25.1 0.2 multiply_convert_fusion
  25.3 2.1 %collective-permute-start.6 = (f16[8,2,32,128]{3,2,1,0:T(8,128)(2,1)S(1)}, f16[8,2,32,128]{3,2,1,0:T(8,128)(2,1)S(1)}, u32[]{:S(2)}, u32[]{:S(2)}) collective-permute-start(f16[8,2,32,128]{3,2,1,0:T(8,128)(2,1)S(1)} %multiply_convert_fusion), channel_id=1, source_target_pairs={{0,2},{1,3},{2,0},{3,1},{4,5},{5,4},{6,7},{7,6},{8,10},{9,11},{10,... | collective-permute-start | bytes 393224 | tf_op jit(solution)/shard_map/ppermute | solution.py:410
  27.5 1.7 %collective-permute-done.8 = bf16[1,6,32,512]{3,2,1,0:T(8,128)(2,1)S(1)} collective-permute-done((bf16[1,6,32,512]{3,2,1,0:T(8,128)(2,1)S(1)}, bf16[1,6,32,512]{3,2,1,0:T(8,128)(2,1)S(1)}, u32[]{:S(2)}, u32[]{:S(2)}) %collective-permute-start.8) | collective-permute-done | bytes 196640 | tf_op jit(solution)/shard_map/ppermute | solution.py:387
  29.2 0.0 collective-permute-done.7
  29.2 0.0 copy-start.1
  29.2 3.5 %near.5.refs_3_ = f32[512,512]{1,0:T(8,128)S(1)} custom-call(f32[9,16,128]{2,1,0:T(8,128)S(1)} %get-tuple-element.34.refs_0_, bf16[4,4,32,512]{3,2,1,0:T(8,128)(2,1)S(1)} %bitcast.12, bf16[4,1,32,512]{3,2,1,0:T(8,128)(2,1)S(1)} %get-tuple-element.56.refs_2_, bf16[4,1,32,512]{3,2,1,0:T(8,128)(2,1)S(1)} %get-tuple-element.55.refs_3_, ...), custom_call_target="tpu_custom_call" | custom-call | flops 3221225472 | bytes 4194304 | tf_op jit(solution)/shard_map/near/pallas_call | solution.py:365
  32.7 0.0 copy-start
  32.7 0.0 collective-permute-done.6
  32.7 0.2 fusion.8.refs_2_
  32.9 0.1 collective-permute-start.9
  33.0 0.0 copy-done.1
  33.0 1.3 %spread.2.refs_3_ = f32[512,512]{1,0:T(8,128)S(1)} custom-call(f32[2,16,2048]{2,1,0:T(8,128)S(1)} %get-tuple-element.26.refs_0_, bf16[2,1024,256]{2,1,0:T(8,128)(2,1)S(1)} %copy-done.1, bf16[8,2,32,128]{3,2,1,0:T(8,128)(2,1)S(1)} %fusion.8.refs_2_, f32[512,512]{1,0:T(8,128)S(1)} %near.5.refs_3_), custom_call_target="tpu_custom_call" | custom-call | flops 1073741824 | bytes 5242880 | tf_op jit(solution)/shard_map/spread/pallas_call | solution.py:273
  34.3 0.1 collective-permute-done.9.refs_2_
  34.3 0.0 copy-done
  34.3 2.2 %spread.3 = f32[512,512]{1,0:T(8,128)} custom-call(f32[2,16,2048]{2,1,0:T(8,128)S(1)} %get-tuple-element.26.refs_0_, bf16[2,1024,256]{2,1,0:T(8,128)(2,1)S(1)} %copy-done, bf16[8,2,32,128]{3,2,1,0:T(8,128)(2,1)S(1)} %collective-permute-done.9.refs_2_, f32[512,512]{1,0:T(8,128)S(1)} %spread.2.refs_3_), custom_call_target="tpu_custom_call" | custom-call | flops 1073741824 | bytes 5242880 | tf_op jit(solution)/shard_map/spread/pallas_call | solution.py:273
  (6 shorter events, 0.1 us)
Async XLA Ops:
  5.9 1.7 %collective-permute-start = (f32[8,2,32,128]{3,2,1,0:T(8,128)S(1)}, f32[8,2,32,128]{3,2,1,0:T(8,128)S(1)}, u32[]{:S(2)}, u32[]{:S(2)}) collective-permute-start(f32[8,2,32,128]{3,2,1,0:T(8,128)S(1)} %get-tuple-element.29), channel_id=1, source_target_pairs={{0,4},{1,5},{2,6},{3,7},{4,0},{5,1},{6,2},{7,3},{8,12},{9,13},{10,... | collective-permute-start | bytes 786440 | tf_op jit(solution)/shard_map/ppermute | solution.py:410
  7.7 6.6 %collective-permute-start.1 = (f16[8,2,32,128]{3,2,1,0:T(8,128)(2,1)S(1)}, f16[8,2,32,128]{3,2,1,0:T(8,128)(2,1)S(1)}, u32[]{:S(2)}, u32[]{:S(2)}) collective-permute-start(f16[8,2,32,128]{3,2,1,0:T(8,128)(2,1)S(1)} %get-tuple-element.31), channel_id=1, source_target_pairs={{0,8},{1,9},{2,10},{3,11},{4,20},{5,21},{6,22},{7,23},{8,0},{9,1},... | collective-permute-start | bytes 393224 | tf_op jit(solution)/shard_map/ppermute | solution.py:410
  10.6 10.4 %collective-permute-start.5 = (bf16[4,1,32,512]{3,2,1,0:T(8,128)(2,1)S(1)}, bf16[4,1,32,512]{3,2,1,0:T(8,128)(2,1)S(1)}, u32[]{:S(2)}, u32[]{:S(2)}) collective-permute-start(bf16[4,1,32,512]{3,2,1,0:T(8,128)(2,1)S(1)} %slice_select_fusion), channel_id=1, source_target_pairs={{0,3},{1,2},{2,1},{3,0},{4,7},{5,6},{6,5},{7,4},{8,11},{9,10},{10,... | collective-permute-start | bytes 393224 | tf_op jit(solution)/shard_map/ppermute | solution.py:387
  14.4 5.0 %collective-permute-start.2 = (f16[8,2,32,128]{3,2,1,0:T(8,128)(2,1)S(1)}, f16[8,2,32,128]{3,2,1,0:T(8,128)(2,1)S(1)}, u32[]{:S(2)}, u32[]{:S(2)}) collective-permute-start(f16[8,2,32,128]{3,2,1,0:T(8,128)(2,1)S(1)} %multiply_convert_fusion.2), channel_id=1, source_target_pairs={{0,16},{1,17},{2,18},{3,19},{4,12},{5,13},{6,14},{7,15},{8,24},{9,... | collective-permute-start | bytes 393224 | tf_op jit(solution)/shard_map/ppermute | solution.py:410
  16.0 5.0 %collective-permute-start.4 = (bf16[4,1,32,512]{3,2,1,0:T(8,128)(2,1)S(1)}, bf16[4,1,32,512]{3,2,1,0:T(8,128)(2,1)S(1)}, u32[]{:S(2)}, u32[]{:S(2)}) collective-permute-start(bf16[4,1,32,512]{3,2,1,0:T(8,128)(2,1)S(1)} %slice_select_fusion.1), channel_id=1, source_target_pairs={{0,1},{1,0},{2,3},{3,2},{4,5},{5,4},{6,7},{7,6},{8,9},{9,8},{10,11... | collective-permute-start | bytes 393224 | tf_op jit(solution)/shard_map/ppermute | solution.py:384
  19.6 5.5 %collective-permute-start.3 = (f16[8,2,32,128]{3,2,1,0:T(8,128)(2,1)S(1)}, f16[8,2,32,128]{3,2,1,0:T(8,128)(2,1)S(1)}, u32[]{:S(2)}, u32[]{:S(2)}) collective-permute-start(f16[8,2,32,128]{3,2,1,0:T(8,128)(2,1)S(1)} %multiply_convert_fusion.1), channel_id=1, source_target_pairs={{0,1},{1,0},{2,3},{3,2},{4,6},{5,7},{6,4},{7,5},{8,9},{9,8},{10,11... | collective-permute-start | bytes 393224 | tf_op jit(solution)/shard_map/ppermute | solution.py:410
  21.1 8.1 %collective-permute-start.8 = (bf16[1,6,32,512]{3,2,1,0:T(8,128)(2,1)S(1)}, bf16[1,6,32,512]{3,2,1,0:T(8,128)(2,1)S(1)}, u32[]{:S(2)}, u32[]{:S(2)}) collective-permute-start(bf16[1,6,32,512]{3,2,1,0:T(8,128)(2,1)S(1)} %get-tuple-element.53), channel_id=1, source_target_pairs={{0,28},{4,8},{8,4},{12,16},{16,12},{20,24},{24,20},{28,0},{1,29},{... | collective-permute-start | bytes 589832 | tf_op jit(solution)/shard_map/ppermute | solution.py:387
  22.4 6.8 %collective-permute-start.7 = (bf16[1,6,32,512]{3,2,1,0:T(8,128)(2,1)S(1)}, bf16[1,6,32,512]{3,2,1,0:T(8,128)(2,1)S(1)}, u32[]{:S(2)}, u32[]{:S(2)}) collective-permute-start(bf16[1,6,32,512]{3,2,1,0:T(8,128)(2,1)S(1)} %get-tuple-element.54), channel_id=1, source_target_pairs={{0,4},{4,0},{8,12},{12,8},{16,20},{20,16},{24,28},{28,24},{1,5},{5... | collective-permute-start | bytes 589832 | tf_op jit(solution)/shard_map/ppermute | solution.py:384
  25.3 7.4 %collective-permute-start.6 = (f16[8,2,32,128]{3,2,1,0:T(8,128)(2,1)S(1)}, f16[8,2,32,128]{3,2,1,0:T(8,128)(2,1)S(1)}, u32[]{:S(2)}, u32[]{:S(2)}) collective-permute-start(f16[8,2,32,128]{3,2,1,0:T(8,128)(2,1)S(1)} %multiply_convert_fusion), channel_id=1, source_target_pairs={{0,2},{1,3},{2,0},{3,1},{4,5},{5,4},{6,7},{7,6},{8,10},{9,11},{10,... | collective-permute-start | bytes 393224 | tf_op jit(solution)/shard_map/ppermute | solution.py:410
  29.2 3.8 %copy-start.1 = (bf16[2,1024,256]{2,1,0:T(8,128)(2,1)S(1)}, bf16[2,1024,256]{2,1,0:T(8,128)(2,1)}, u32[]{:S(2)}) copy-start(bf16[2,1024,256]{2,1,0:T(8,128)(2,1)} %get-tuple-element.45.refs_1_) | copy-start | bytes 3145732
  32.7 1.6 %copy-start = (bf16[2,1024,256]{2,1,0:T(8,128)(2,1)S(1)}, bf16[2,1024,256]{2,1,0:T(8,128)(2,1)}, u32[]{:S(2)}) copy-start(bf16[2,1024,256]{2,1,0:T(8,128)(2,1)} %get-tuple-element.27.refs_1_) | copy-start | bytes 3145732
  32.9 1.4 %collective-permute-start.9 = (bf16[8,2,32,128]{3,2,1,0:T(8,128)(2,1)S(1)}, bf16[8,2,32,128]{3,2,1,0:T(8,128)(2,1)S(1)}, u32[]{:S(2)}, u32[]{:S(2)}) collective-permute-start(bf16[8,2,32,128]{3,2,1,0:T(8,128)(2,1)S(1)} %fusion.8.refs_2_), channel_id=1, source_target_pairs={{0,4},{1,5},{2,6},{3,7},{4,0},{5,1},{6,2},{7,3},{8,12},{9,13},{10,... | collective-permute-start | bytes 393224 | tf_op jit(solution)/shard_map/ppermute | solution.py:410

commit v5 on v4

--- a/solution.py
+++ b/solution.py
@@ -184,13 +184,14 @@
         if t > 0:
             add(t - 1)
     add(count - 1)
-    for c in small[4:] + stores:
-        c.wait()
+    small[4].wait()
     cols = shift.shape[2]
     for o in range(mask_ref.shape[0]):
         for p in range(n):
             chosen = jnp.full((1, LANES), contact[p // cols, p % cols, o], jnp.int32)
             mask_ref[o, p : p + 1, :] = chosen.astype(F32)
+    for c in small[5:] + stores:
+        c.wait()
 
 
 def in_hbm(*arrays):

time: 36.8 us -> 36.7 us (level)
  no operation moved by 1% of the time
where the time goes in v5:
time: 36.7 us; the launch traced here: 36.5 us
  Pallas kernels  16.1 us (44%)
  starting transfers between devices  15.4 us (42%)
  waiting for transfers between devices  3.97 us (11%)
  other arithmetic  0.89 us (2%)
    ppermute x6, starting transfers between devices, exchange(): return lax.ppermute(value, ('row', 'col'), pairs)  8.66 us
    pallas_call x3, Pallas kernels, near_field(): pl.pallas_call(body, in_specs=specs + [VMEM] * after, out_specs=[VMEM] *...  6.73 us
    pallas_call x1, Pallas kernels, project(): pl.pallas_call(body, in_specs=[HBM] * 7, out_specs=[VMEM] * 2 + [HBM] * 2...  5.84 us
    ppermute x2, starting transfers between devices, second(): return lax.ppermute(jnp.where(odd, high, low), axis, outer)  4.94 us
    pallas_call x2, Pallas kernels, spread(): pl.pallas_call(body, in_specs=[VMEM] * 4, out_specs=VMEM, out_shape=jax.S...  3.49 us
    ppermute x6, waiting for transfers between devices, exchange(): return lax.ppermute(value, ('row', 'col'), pairs)  2.25 us
    ppermute x2, starting transfers between devices, first(): return lax.ppermute(jnp.where(odd, low, high), axis, inner)  1.82 us
    ppermute x2, waiting for transfers between devices, second(): return lax.ppermute(jnp.where(odd, high, low), axis, outer)  1.71 us
  transfers between devices with their start and end apart: 10, of which 4 were waited for; matrix products, arithmetic and copies ran while one was open for 2% of the time, Pallas kernels for 22%

profile of v5, /device:TPU:0, one launch (start us, length us, event | category | flops | bytes accessed | tf_op | source)
XLA Modules:
  0.0 36.5 jit_solution(13340915044509240858)
XLA Ops:
  0.0 5.8 %project.1 = (f32[8,2,32,128]{3,2,1,0:T(8,128)S(1)}, f32[8,2,32,128]{3,2,1,0:T(8,128)S(1)}, bf16[2,1024,256]{2,1,0:T(8,128)(2,1)}, bf16[2,1024,256]{2,1,0:T(8,12...) custom-call(bf16[512,512]{1,0:T(8,128)(2,1)} %bitcast.15, ...), custom_call_target="tpu_custom_call" | custom-call | flops 2147483648 | bytes 5242880 | tf_op jit(solution)/shard_map/project/pallas_call | solution.py:212
  5.8 0.5 %collective-permute-start = (f32[8,2,32,128]{3,2,1,0:T(8,128)S(1)}, f32[8,2,32,128]{3,2,1,0:T(8,128)S(1)}, u32[]{:S(2)}, u32[]{:S(2)}) collective-permute-start(f32[8,2,32,128]{3,2,1,0:T(8,128)S(1)} %get-tuple-element.29), channel_id=1, source_target_pairs={{0,4},{1,5},{2,6},{3,7},{4,0},{5,1},{6,2},{7,3},{8,12},{9,13},{10,... | collective-permute-start | bytes 786440 | tf_op jit(solution)/shard_map/ppermute | solution.py:411
  6.4 1.1 %collective-permute-done = f32[8,2,32,128]{3,2,1,0:T(8,128)S(1)} collective-permute-done((f32[8,2,32,128]{3,2,1,0:T(8,128)S(1)}, f32[8,2,32,128]{3,2,1,0:T(8,128)S(1)}, u32[]{:S(2)}, u32[]{:S(2)}) %collective-permute-start) | collective-permute-done | bytes 262176 | tf_op jit(solution)/shard_map/ppermute | solution.py:411
  7.5 0.1 multiply_convert_fusion.3
  7.6 2.9 %collective-permute-start.1 = (f16[8,2,32,128]{3,2,1,0:T(8,128)(2,1)S(1)}, f16[8,2,32,128]{3,2,1,0:T(8,128)(2,1)S(1)}, u32[]{:S(2)}, u32[]{:S(2)}) collective-permute-start(f16[8,2,32,128]{3,2,1,0:T(8,128)(2,1)S(1)} %get-tuple-element.31), channel_id=1, source_target_pairs={{0,8},{1,9},{2,10},{3,11},{4,20},{5,21},{6,22},{7,23},{8,0},{9,1},... | collective-permute-start | bytes 393224 | tf_op jit(solution)/shard_map/ppermute | solution.py:411
  10.6 3.7 %collective-permute-start.5 = (bf16[4,1,32,512]{3,2,1,0:T(8,128)(2,1)S(1)}, bf16[4,1,32,512]{3,2,1,0:T(8,128)(2,1)S(1)}, u32[]{:S(2)}, u32[]{:S(2)}) collective-permute-start(bf16[4,1,32,512]{3,2,1,0:T(8,128)(2,1)S(1)} %slice_select_fusion), channel_id=1, source_target_pairs={{0,3},{1,2},{2,1},{3,0},{4,7},{5,6},{6,5},{7,4},{8,11},{9,10},{10,... | collective-permute-start | bytes 393224 | tf_op jit(solution)/shard_map/ppermute | solution.py:388
  14.2 0.0 collective-permute-done.1
  14.2 0.1 multiply_convert_fusion.2
  14.3 1.6 %collective-permute-start.2 = (f16[8,2,32,128]{3,2,1,0:T(8,128)(2,1)S(1)}, f16[8,2,32,128]{3,2,1,0:T(8,128)(2,1)S(1)}, u32[]{:S(2)}, u32[]{:S(2)}) collective-permute-start(f16[8,2,32,128]{3,2,1,0:T(8,128)(2,1)S(1)} %multiply_convert_fusion.2), channel_id=1, source_target_pairs={{0,16},{1,17},{2,18},{3,19},{4,12},{5,13},{6,14},{7,15},{8,24},{9,... | collective-permute-start | bytes 393224 | tf_op jit(solution)/shard_map/ppermute | solution.py:411
  15.9 1.4 %collective-permute-start.4 = (bf16[4,1,32,512]{3,2,1,0:T(8,128)(2,1)S(1)}, bf16[4,1,32,512]{3,2,1,0:T(8,128)(2,1)S(1)}, u32[]{:S(2)}, u32[]{:S(2)}) collective-permute-start(bf16[4,1,32,512]{3,2,1,0:T(8,128)(2,1)S(1)} %slice_select_fusion.1), channel_id=1, source_target_pairs={{0,1},{1,0},{2,3},{3,2},{4,5},{5,4},{6,7},{7,6},{8,9},{9,8},{10,11... | collective-permute-start | bytes 393224 | tf_op jit(solution)/shard_map/ppermute | solution.py:385
  17.4 2.0 %near.3 = (f32[512,512]{1,0:T(8,128)S(1)}, bf16[6,2,2,256,256]{4,3,2,1,0:T(8,128)(2,1)S(1)}) custom-call(f32[9,16,128]{2,1,0:T(8,128)S(1)} %get-tuple-element.34.refs_0_, bf16[4,4,32,512]{3,2,1,0:T(8,128)(2,1)S(1)} %bitcast.10, bf16[1,2,2,256,256]{4,3,2,1,0:T(8,128)(2,1)S(1)} %get-tuple-element.36.refs_2_, bf16[9,2,2,256,256]{4,3,2,1,0:T(8,128)(2,1)} %refs_3_.1), custom_call_target="tpu_custom_call" | custom-call | flops 536870912 | bytes 4194304 | tf_op jit(solution)/shard_map/near/pallas_call | solution.py:366
  19.4 0.0 collective-permute-done.2
  19.4 0.2 multiply_convert_fusion.1
  19.5 1.4 %collective-permute-start.3 = (f16[8,2,32,128]{3,2,1,0:T(8,128)(2,1)S(1)}, f16[8,2,32,128]{3,2,1,0:T(8,128)(2,1)S(1)}, u32[]{:S(2)}, u32[]{:S(2)}) collective-permute-start(f16[8,2,32,128]{3,2,1,0:T(8,128)(2,1)S(1)} %multiply_convert_fusion.1), channel_id=1, source_target_pairs={{0,1},{1,0},{2,3},{3,2},{4,6},{5,7},{6,4},{7,5},{8,9},{9,8},{10,11... | collective-permute-start | bytes 393224 | tf_op jit(solution)/shard_map/ppermute | solution.py:411
  21.0 0.0 collective-permute-done.5
  21.0 0.0 collective-permute-done.4
  21.0 0.1 broadcast_select_fusion.2
  21.1 1.3 %collective-permute-start.8 = (bf16[1,6,32,512]{3,2,1,0:T(8,128)(2,1)S(1)}, bf16[1,6,32,512]{3,2,1,0:T(8,128)(2,1)S(1)}, u32[]{:S(2)}, u32[]{:S(2)}) collective-permute-start(bf16[1,6,32,512]{3,2,1,0:T(8,128)(2,1)S(1)} %get-tuple-element.53), channel_id=1, source_target_pairs={{0,28},{4,8},{8,4},{12,16},{16,12},{20,24},{24,20},{28,0},{1,29},{... | collective-permute-start | bytes 589832 | tf_op jit(solution)/shard_map/ppermute | solution.py:388
  22.4 0.4 %collective-permute-start.7 = (bf16[1,6,32,512]{3,2,1,0:T(8,128)(2,1)S(1)}, bf16[1,6,32,512]{3,2,1,0:T(8,128)(2,1)S(1)}, u32[]{:S(2)}, u32[]{:S(2)}) collective-permute-start(bf16[1,6,32,512]{3,2,1,0:T(8,128)(2,1)S(1)} %get-tuple-element.54), channel_id=1, source_target_pairs={{0,4},{4,0},{8,12},{12,8},{16,20},{20,16},{24,28},{28,24},{1,5},{5... | collective-permute-start | bytes 589832 | tf_op jit(solution)/shard_map/ppermute | solution.py:385
  22.8 1.3 %near.4.refs_7_ = f32[512,512]{1,0:T(8,128)S(1)} custom-call(f32[9,16,128]{2,1,0:T(8,128)S(1)} %get-tuple-element.34.refs_0_, bf16[4,4,32,512]{3,2,1,0:T(8,128)(2,1)S(1)} %bitcast.11, bf16[4,1,32,512]{3,2,1,0:T(8,128)(2,1)S(1)} %get-tuple-element.56.refs_2_, bf16[4,1,32,512]{3,2,1,0:T(8,128)(2,1)S(1)} %get-tuple-element.55.refs_3_, ...), custom_call_target="tpu_custom_call" | custom-call | flops 1073741824 | bytes 4194304 | tf_op jit(solution)/shard_map/near/pallas_call | solution.py:366
  24.1 1.0 %collective-permute-done.3 = f16[8,2,32,128]{3,2,1,0:T(8,128)(2,1)S(1)} collective-permute-done((f16[8,2,32,128]{3,2,1,0:T(8,128)(2,1)S(1)}, f16[8,2,32,128]{3,2,1,0:T(8,128)(2,1)S(1)}, u32[]{:S(2)}, u32[]{:S(2)}) %collective-permute-start.3) | collective-permute-done | bytes 131104 | tf_op jit(solution)/shard_map/ppermute | solution.py:411
  25.1 0.2 multiply_convert_fusion
  25.3 2.1 %collective-permute-start.6 = (f16[8,2,32,128]{3,2,1,0:T(8,128)(2,1)S(1)}, f16[8,2,32,128]{3,2,1,0:T(8,128)(2,1)S(1)}, u32[]{:S(2)}, u32[]{:S(2)}) collective-permute-start(f16[8,2,32,128]{3,2,1,0:T(8,128)(2,1)S(1)} %multiply_convert_fusion), channel_id=1, source_target_pairs={{0,2},{1,3},{2,0},{3,1},{4,5},{5,4},{6,7},{7,6},{8,10},{9,11},{10,... | collective-permute-start | bytes 393224 | tf_op jit(solution)/shard_map/ppermute | solution.py:411
  27.4 1.7 %collective-permute-done.8 = bf16[1,6,32,512]{3,2,1,0:T(8,128)(2,1)S(1)} collective-permute-done((bf16[1,6,32,512]{3,2,1,0:T(8,128)(2,1)S(1)}, bf16[1,6,32,512]{3,2,1,0:T(8,128)(2,1)S(1)}, u32[]{:S(2)}, u32[]{:S(2)}) %collective-permute-start.8) | collective-permute-done | bytes 196640 | tf_op jit(solution)/shard_map/ppermute | solution.py:388
  29.1 0.0 collective-permute-done.7
  29.2 0.0 copy-start.1
  29.2 3.5 %near.5.refs_3_ = f32[512,512]{1,0:T(8,128)S(1)} custom-call(f32[9,16,128]{2,1,0:T(8,128)S(1)} %get-tuple-element.34.refs_0_, bf16[4,4,32,512]{3,2,1,0:T(8,128)(2,1)S(1)} %bitcast.12, bf16[4,1,32,512]{3,2,1,0:T(8,128)(2,1)S(1)} %get-tuple-element.56.refs_2_, bf16[4,1,32,512]{3,2,1,0:T(8,128)(2,1)S(1)} %get-tuple-element.55.refs_3_, ...), custom_call_target="tpu_custom_call" | custom-call | flops 3221225472 | bytes 4194304 | tf_op jit(solution)/shard_map/near/pallas_call | solution.py:366
  32.7 0.0 copy-start
  32.7 0.0 collective-permute-done.6
  32.7 0.2 fusion.8.refs_2_
  32.9 0.1 collective-permute-start.9
  33.0 0.0 copy-done.1
  33.0 1.3 %spread.2.refs_3_ = f32[512,512]{1,0:T(8,128)S(1)} custom-call(f32[2,16,2048]{2,1,0:T(8,128)S(1)} %get-tuple-element.26.refs_0_, bf16[2,1024,256]{2,1,0:T(8,128)(2,1)S(1)} %copy-done.1, bf16[8,2,32,128]{3,2,1,0:T(8,128)(2,1)S(1)} %fusion.8.refs_2_, f32[512,512]{1,0:T(8,128)S(1)} %near.5.refs_3_), custom_call_target="tpu_custom_call" | custom-call | flops 1073741824 | bytes 5242880 | tf_op jit(solution)/shard_map/spread/pallas_call | solution.py:274
  34.2 0.1 collective-permute-done.9.refs_2_
  34.3 0.0 copy-done
  34.3 2.2 %spread.3 = f32[512,512]{1,0:T(8,128)} custom-call(f32[2,16,2048]{2,1,0:T(8,128)S(1)} %get-tuple-element.26.refs_0_, bf16[2,1024,256]{2,1,0:T(8,128)(2,1)S(1)} %copy-done, bf16[8,2,32,128]{3,2,1,0:T(8,128)(2,1)S(1)} %collective-permute-done.9.refs_2_, f32[512,512]{1,0:T(8,128)S(1)} %spread.2.refs_3_), custom_call_target="tpu_custom_call" | custom-call | flops 1073741824 | bytes 5242880 | tf_op jit(solution)/shard_map/spread/pallas_call | solution.py:274
  (6 shorter events, 0.1 us)
Async XLA Ops:
  5.8 1.7 %collective-permute-start = (f32[8,2,32,128]{3,2,1,0:T(8,128)S(1)}, f32[8,2,32,128]{3,2,1,0:T(8,128)S(1)}, u32[]{:S(2)}, u32[]{:S(2)}) collective-permute-start(f32[8,2,32,128]{3,2,1,0:T(8,128)S(1)} %get-tuple-element.29), channel_id=1, source_target_pairs={{0,4},{1,5},{2,6},{3,7},{4,0},{5,1},{6,2},{7,3},{8,12},{9,13},{10,... | collective-permute-start | bytes 786440 | tf_op jit(solution)/shard_map/ppermute | solution.py:411
  7.6 6.6 %collective-permute-start.1 = (f16[8,2,32,128]{3,2,1,0:T(8,128)(2,1)S(1)}, f16[8,2,32,128]{3,2,1,0:T(8,128)(2,1)S(1)}, u32[]{:S(2)}, u32[]{:S(2)}) collective-permute-start(f16[8,2,32,128]{3,2,1,0:T(8,128)(2,1)S(1)} %get-tuple-element.31), channel_id=1, source_target_pairs={{0,8},{1,9},{2,10},{3,11},{4,20},{5,21},{6,22},{7,23},{8,0},{9,1},... | collective-permute-start | bytes 393224 | tf_op jit(solution)/shard_map/ppermute | solution.py:411
  10.6 10.4 %collective-permute-start.5 = (bf16[4,1,32,512]{3,2,1,0:T(8,128)(2,1)S(1)}, bf16[4,1,32,512]{3,2,1,0:T(8,128)(2,1)S(1)}, u32[]{:S(2)}, u32[]{:S(2)}) collective-permute-start(bf16[4,1,32,512]{3,2,1,0:T(8,128)(2,1)S(1)} %slice_select_fusion), channel_id=1, source_target_pairs={{0,3},{1,2},{2,1},{3,0},{4,7},{5,6},{6,5},{7,4},{8,11},{9,10},{10,... | collective-permute-start | bytes 393224 | tf_op jit(solution)/shard_map/ppermute | solution.py:388
  14.3 5.0 %collective-permute-start.2 = (f16[8,2,32,128]{3,2,1,0:T(8,128)(2,1)S(1)}, f16[8,2,32,128]{3,2,1,0:T(8,128)(2,1)S(1)}, u32[]{:S(2)}, u32[]{:S(2)}) collective-permute-start(f16[8,2,32,128]{3,2,1,0:T(8,128)(2,1)S(1)} %multiply_convert_fusion.2), channel_id=1, source_target_pairs={{0,16},{1,17},{2,18},{3,19},{4,12},{5,13},{6,14},{7,15},{8,24},{9,... | collective-permute-start | bytes 393224 | tf_op jit(solution)/shard_map/ppermute | solution.py:411
  15.9 5.0 %collective-permute-start.4 = (bf16[4,1,32,512]{3,2,1,0:T(8,128)(2,1)S(1)}, bf16[4,1,32,512]{3,2,1,0:T(8,128)(2,1)S(1)}, u32[]{:S(2)}, u32[]{:S(2)}) collective-permute-start(bf16[4,1,32,512]{3,2,1,0:T(8,128)(2,1)S(1)} %slice_select_fusion.1), channel_id=1, source_target_pairs={{0,1},{1,0},{2,3},{3,2},{4,5},{5,4},{6,7},{7,6},{8,9},{9,8},{10,11... | collective-permute-start | bytes 393224 | tf_op jit(solution)/shard_map/ppermute | solution.py:385
  19.5 5.5 %collective-permute-start.3 = (f16[8,2,32,128]{3,2,1,0:T(8,128)(2,1)S(1)}, f16[8,2,32,128]{3,2,1,0:T(8,128)(2,1)S(1)}, u32[]{:S(2)}, u32[]{:S(2)}) collective-permute-start(f16[8,2,32,128]{3,2,1,0:T(8,128)(2,1)S(1)} %multiply_convert_fusion.1), channel_id=1, source_target_pairs={{0,1},{1,0},{2,3},{3,2},{4,6},{5,7},{6,4},{7,5},{8,9},{9,8},{10,11... | collective-permute-start | bytes 393224 | tf_op jit(solution)/shard_map/ppermute | solution.py:411
  21.1 8.1 %collective-permute-start.8 = (bf16[1,6,32,512]{3,2,1,0:T(8,128)(2,1)S(1)}, bf16[1,6,32,512]{3,2,1,0:T(8,128)(2,1)S(1)}, u32[]{:S(2)}, u32[]{:S(2)}) collective-permute-start(bf16[1,6,32,512]{3,2,1,0:T(8,128)(2,1)S(1)} %get-tuple-element.53), channel_id=1, source_target_pairs={{0,28},{4,8},{8,4},{12,16},{16,12},{20,24},{24,20},{28,0},{1,29},{... | collective-permute-start | bytes 589832 | tf_op jit(solution)/shard_map/ppermute | solution.py:388
  22.4 6.8 %collective-permute-start.7 = (bf16[1,6,32,512]{3,2,1,0:T(8,128)(2,1)S(1)}, bf16[1,6,32,512]{3,2,1,0:T(8,128)(2,1)S(1)}, u32[]{:S(2)}, u32[]{:S(2)}) collective-permute-start(bf16[1,6,32,512]{3,2,1,0:T(8,128)(2,1)S(1)} %get-tuple-element.54), channel_id=1, source_target_pairs={{0,4},{4,0},{8,12},{12,8},{16,20},{20,16},{24,28},{28,24},{1,5},{5... | collective-permute-start | bytes 589832 | tf_op jit(solution)/shard_map/ppermute | solution.py:385
  25.3 7.4 %collective-permute-start.6 = (f16[8,2,32,128]{3,2,1,0:T(8,128)(2,1)S(1)}, f16[8,2,32,128]{3,2,1,0:T(8,128)(2,1)S(1)}, u32[]{:S(2)}, u32[]{:S(2)}) collective-permute-start(f16[8,2,32,128]{3,2,1,0:T(8,128)(2,1)S(1)} %multiply_convert_fusion), channel_id=1, source_target_pairs={{0,2},{1,3},{2,0},{3,1},{4,5},{5,4},{6,7},{7,6},{8,10},{9,11},{10,... | collective-permute-start | bytes 393224 | tf_op jit(solution)/shard_map/ppermute | solution.py:411
  29.2 3.8 %copy-start.1 = (bf16[2,1024,256]{2,1,0:T(8,128)(2,1)S(1)}, bf16[2,1024,256]{2,1,0:T(8,128)(2,1)}, u32[]{:S(2)}) copy-start(bf16[2,1024,256]{2,1,0:T(8,128)(2,1)} %get-tuple-element.45.refs_1_) | copy-start | bytes 3145732
  32.7 1.6 %copy-start = (bf16[2,1024,256]{2,1,0:T(8,128)(2,1)S(1)}, bf16[2,1024,256]{2,1,0:T(8,128)(2,1)}, u32[]{:S(2)}) copy-start(bf16[2,1024,256]{2,1,0:T(8,128)(2,1)} %get-tuple-element.27.refs_1_) | copy-start | bytes 3145732
  32.9 1.4 %collective-permute-start.9 = (bf16[8,2,32,128]{3,2,1,0:T(8,128)(2,1)S(1)}, bf16[8,2,32,128]{3,2,1,0:T(8,128)(2,1)S(1)}, u32[]{:S(2)}, u32[]{:S(2)}) collective-permute-start(bf16[8,2,32,128]{3,2,1,0:T(8,128)(2,1)S(1)} %fusion.8.refs_2_), channel_id=1, source_target_pairs={{0,4},{1,5},{2,6},{3,7},{4,0},{5,1},{6,2},{7,3},{8,12},{9,13},{10,... | collective-permute-start | bytes 393224 | tf_op jit(solution)/shard_map/ppermute | solution.py:411
